TPU v7x, 512 devices: a whole 4x8x8 slice. The times are simulated.
512 devices in a mesh: group: 64 (over z_hi, y, x), tensor: 8 (over z_lo, core).
Axes of the slice: x: 4, y: 8, z: 8 (z_hi: 2, z_lo: 4; z = z_hi * 4 + z_lo), core: 2. Of those that a mesh axis runs over, the one named last changes fastest.
Arguments:
- queries: bfloat16 [1024, 2, 8192], P('group', None, 'tensor'), may hold values from -42 to 42
- new_kv: bfloat16 [1024, 2, 2, 1024], P('group', None, None, 'tensor'), may hold values from -42 to 42
- own_kv: bfloat16 [1024, 256, 2, 1024], P('group', None, None, 'tensor'), may hold values from -42 to 42
- prefix_kv: bfloat16 [64, 4096, 2, 8, 128], P('group', 'tensor'), may hold values from -15 to 15
- owner: int32 [64], replicated, may hold values from 0 to 63, as said below
- parent: int32 [1024], P('group'), may hold values from 0 to 63, as said below
- own_len: int32 [1024], P('group'), may hold values from 2 to 256, as said below
Outputs:
- attended: bfloat16 [1024, 2, 8192], P('group', None, 'tensor')
Inputs may be any that keep to these rules, and one draw needn't show every extreme that they name: `owner`: each group holds exactly one node's prefix. The owner of a row's parent lies 1 to 6 groups before the row's group, counted cyclically; in every draw some row lies exactly 6 groups after it. `own_len`: some row has all 256 slots live.
All inputs are finite; a program needn't handle non-finite values.
Results may differ from a plain program's by a relative error of at most 0.015.
Values may be sent and summed in bfloat16 or wider, within the bound.
No kernel may reach another device: no remote copies, remote signals or barrier semaphores. Data moves between devices by JAX's collectives and lax.ppermute only.
A program may use at most 64 MiB of HBM per device.

v0:
```python
import jax
import jax.numpy as jnp
from jax import lax
from jax.sharding import PartitionSpec as P

MAXFAN = 6


def passed_along(x, axis, by):
    peers = lax.axis_size(axis)
    return lax.ppermute(x, axis, [(i, (i + by) % peers) for i in range(peers)])


def prefix_partial(grouped, prefix_keys, prefix_values):
    key_count = prefix_keys.shape[0]
    kv_local = prefix_keys.shape[1]
    head_dim = prefix_keys.shape[2]
    block_len = 1024
    scaling = head_dim ** (-0.5)
    key_blocks = prefix_keys.reshape(key_count // block_len, block_len, kv_local, head_dim)
    value_blocks = prefix_values.reshape(key_count // block_len, block_len, kv_local, head_dim)
    lead_shape = grouped.shape[:4]

    def advance(carry, block_pair):
        maxima, totals, summed = carry
        scores = (
            jnp.einsum(
                "rtkjd,pkd->rtkjp", grouped, block_pair[0], preferred_element_type=jnp.float32
            )
            * scaling
        )
        newest = jnp.maximum(maxima, scores.max(-1))
        shrink = jnp.exp(maxima - newest)
        weights = jnp.exp(scores - newest[..., None])
        totals = totals * shrink + weights.sum(-1)
        product = jnp.einsum(
            "rtkjp,pkd->rtkjd",
            weights.astype(jnp.bfloat16),
            block_pair[1],
            preferred_element_type=jnp.float32,
        )
        summed = summed * shrink[..., None] + product
        return ((newest, totals, summed), None)

    initial = (
        jnp.full(lead_shape, -jnp.inf, jnp.float32),
        jnp.zeros(lead_shape, jnp.float32),
        jnp.zeros(lead_shape + (head_dim,), jnp.float32),
    )
    result, _ = lax.scan(advance, initial, (key_blocks, value_blocks))
    return result


def local_partial(grouped, own_kv, new_kv, own_len):
    row_count, draft, kv_local, per_kv, head_dim = grouped.shape
    scaling = head_dim ** (-0.5)
    own_cache = own_kv.reshape(row_count, own_kv.shape[1], 2, kv_local, head_dim)
    new_cache = new_kv.reshape(row_count, draft, 2, kv_local, head_dim)
    s_own = (
        jnp.einsum(
            "rtkjd,rpkd->rtkjp", grouped, own_cache[:, :, 0], preferred_element_type=jnp.float32
        )
        * scaling
    )
    s_new = (
        jnp.einsum(
            "rtkjd,rukd->rtkju", grouped, new_cache[:, :, 0], preferred_element_type=jnp.float32
        )
        * scaling
    )
    live_mask = jnp.arange(own_cache.shape[1])[None, :] < own_len[:, None]
    s_own = jnp.where(live_mask[:, None, None, None, :], s_own, -jnp.inf)
    causal = jnp.arange(draft)[None, :] <= jnp.arange(draft)[:, None]
    s_new = jnp.where(causal[None, :, None, None, :], s_new, -jnp.inf)
    maxima = jnp.maximum(s_own.max(-1), s_new.max(-1))
    w_own = jnp.exp(s_own - maxima[..., None])
    w_new = jnp.exp(s_new - maxima[..., None])
    totals = w_own.sum(-1) + w_new.sum(-1)
    summed = jnp.einsum(
        "rtkjp,rpkd->rtkjd",
        w_own.astype(jnp.bfloat16),
        own_cache[:, :, 1],
        preferred_element_type=jnp.float32,
    )
    summed = summed + jnp.einsum(
        "rtkju,rukd->rtkjd",
        w_new.astype(jnp.bfloat16),
        new_cache[:, :, 1],
        preferred_element_type=jnp.float32,
    )
    return (maxima, totals, summed)


def merge_parts(first, second):
    maxima = jnp.maximum(first[0], second[0])
    first_scale = jnp.exp(first[0] - maxima)
    second_scale = jnp.exp(second[0] - maxima)
    totals = first[1] * first_scale + second[1] * second_scale
    summed = first[2] * first_scale[..., None] + second[2] * second_scale[..., None]
    return (maxima, totals, summed)


def select_rows(chosen, taken, kept):
    flat_mask = chosen[:, None, None, None]
    return (
        jnp.where(flat_mask, taken[0], kept[0]),
        jnp.where(flat_mask, taken[1], kept[1]),
        jnp.where(flat_mask[..., None], taken[2], kept[2]),
    )


def on_device(queries, new_kv, own_kv, prefix_kv, owner, parent, own_len):
    row_count = queries.shape[0]
    draft = queries.shape[1]
    head_dim = prefix_kv.shape[4]
    kv_local = new_kv.shape[3] // head_dim
    per_kv = queries.shape[2] // (kv_local * head_dim)
    grouped = queries.reshape(row_count, draft, kv_local, per_kv, head_dim)
    regrouped = lax.all_to_all(prefix_kv, "tensor", split_axis=3, concat_axis=1, tiled=True)
    group_count = lax.axis_size("group")
    distance = (lax.axis_index("group") - owner[parent]) % group_count
    lead_shape = grouped.shape[:4]
    gathered = (
        jnp.full(lead_shape, -jnp.inf, jnp.float32),
        jnp.zeros(lead_shape, jnp.float32),
        jnp.zeros(lead_shape + (head_dim,), jnp.float32),
    )
    for offset in range(1, MAXFAN + 1):
        arrived = passed_along(regrouped, "group", offset)
        partial_terms = prefix_partial(grouped, arrived[0, :, 0], arrived[0, :, 1])
        gathered = select_rows(distance == offset, partial_terms, gathered)
    maxima, totals, summed = merge_parts(gathered, local_partial(grouped, own_kv, new_kv, own_len))
    result = summed / totals[..., None]
    return result.astype(jnp.bfloat16).reshape(row_count, draft, kv_local * per_kv * head_dim)


def solution(mesh):
    placed = (
        P("group", None, "tensor"),
        P("group", None, None, "tensor"),
        P("group", None, None, "tensor"),
        P("group", "tensor", None, None, None),
        P(),
        P("group"),
        P("group"),
    )
    return jax.shard_map(
        on_device, mesh=mesh, in_specs=placed, out_specs=P("group", None, "tensor"), check_vma=False
    )
```

profile of v0, /device:TPU:1, one launch (start us, length us, event | category | flops | bytes accessed | tf_op | source)
XLA Modules:
  0.0 630.4 jit_solution(14160457510966574791)
XLA Ops:
  0.0 2.1 copy.99
  2.1 57.3 %all_to_all.18 = bf16[1,512,2,8,128]{4,1,2,0,3:T(8,128)(2,1)S(1)} all-to-all(bf16[1,512,2,8,128]{4,1,2,0,3:T(8,128)(2,1)S(1)} %copy.99), channel_id=1, replica_groups=mesh['group'=64,'tensor'=8] {'tensor'}, dimensions={3} | all-to-all | bytes 4194304 | tf_op jit(solution)/shard_map/all_to_all | solution.py:119
  59.5 1.5 copy.100
  61.0 4.9 collective-permute-start
  66.3 0.5 copy.194
  67.0 1.2 copy-done.2
  68.2 1.1 fusion.144
  69.4 0.4 fusion.145
  69.9 0.7 gather_fusion
  70.6 3.2 collective-permute-start.1
  73.9 3.2 collective-permute-start.2
  77.1 6.5 %collective-permute-start.3 = (bf16[1,4096,2,1,128]{4,1,2,3,0:T(8,128)(2,1)}, bf16[1,4096,2,1,128]{4,1,2,3,0:T(8,128)(2,1)}, u32[]{:S(2)}, u32[]{:S(2)}) collective-permute-start(bf16[1,4096,2,1,128]{4,1,2,3,0:T(8,128)(2,1)} %bitcast.2), channel_id=1, source_target_pairs={{0,24},{8,32},{16,40},{24,48},{32,56},{40,64},{48,72},{56,80},{64,... | collective-permute-start | bytes 6291464 | tf_op jit(solution)/shard_map/ppermute | solution.py:11
  83.6 1.9 collective-permute-start.4
  85.5 80.1 %collective-permute-done = bf16[1,4096,2,1,128]{4,1,2,3,0:T(8,128)(2,1)} collective-permute-done((bf16[1,4096,2,1,128]{4,1,2,3,0:T(8,128)(2,1)}, bf16[1,4096,2,1,128]{4,1,2,3,0:T(8,128)(2,1)}, u32[]{:S(2)}, u32[]{:S(2)}) %collective-permute-start) | collective-permute-done | bytes 2097184 | tf_op jit(solution)/shard_map/ppermute | solution.py:11
  165.6 4.1 collective-permute-start.5
  169.6 1.7 fusion.138
  171.3 10.0 %while.90 = (s32[]{:T(128)}, f32[16,2,1,8]{0,3,1,2:T(8,128)S(1)}, f32[16,2,1,8]{0,3,1,2:T(8,128)S(1)}, f32[16,2,1,8,128]{4,0,3,1,2:T(8,128)}, bf16[4,1024,1,128]...) while((s32[]{:T(128)}, f32[16,2,1,8]{0,3,1,2:T(8,128)S(1)}, ...), condition=%wide.region_3.4_spmd.clone, body=%wide.region_0.3_spmd.clone.sunk | while | flops 135890432 | bytes 4028529 | solution.py:50
  171.7 1.1 fusion.189
  173.6 2.0 fusion.189
  176.3 2.0 fusion.189
  179.0 2.0 fusion.189
  181.4 73.4 %collective-permute-done.1 = bf16[1,4096,2,1,128]{4,1,2,3,0:T(8,128)(2,1)} collective-permute-done((bf16[1,4096,2,1,128]{4,1,2,3,0:T(8,128)(2,1)}, bf16[1,4096,2,1,128]{4,1,2,3,0:T(8,128)(2,1)}, u32[]{:S(2)}, u32[]{:S(2)}) %collective-permute-start.1) | collective-permute-done | bytes 2097184 | tf_op jit(solution)/shard_map/ppermute | solution.py:11
  254.7 1.7 fusion.139
  256.4 10.0 %while.91 = (s32[]{:T(128)}, f32[16,2,1,8]{0,3,1,2:T(8,128)S(1)}, f32[16,2,1,8]{0,3,1,2:T(8,128)S(1)}, f32[16,2,1,8,128]{4,0,3,1,2:T(8,128)}, bf16[4,1024,1,128]...) while((s32[]{:T(128)}, f32[16,2,1,8]{0,3,1,2:T(8,128)S(1)}, ...), condition=%wide.region_7.8_spmd.clone, body=%wide.region_4.7_spmd.clone.sunk | while | flops 135890432 | bytes 4028529 | solution.py:50
  256.8 1.1 fusion.195
  258.2 0.4 fusion.192
  258.6 2.0 fusion.195
  261.4 2.0 fusion.195
  264.1 2.0 fusion.195
  266.4 76.3 %collective-permute-done.2 = bf16[1,4096,2,1,128]{4,1,2,3,0:T(8,128)(2,1)} collective-permute-done((bf16[1,4096,2,1,128]{4,1,2,3,0:T(8,128)(2,1)}, bf16[1,4096,2,1,128]{4,1,2,3,0:T(8,128)(2,1)}, u32[]{:S(2)}, u32[]{:S(2)}) %collective-permute-start.2) | collective-permute-done | bytes 2097184 | tf_op jit(solution)/shard_map/ppermute | solution.py:11
  342.7 1.7 fusion.140
  344.4 10.0 %while.92 = (s32[]{:T(128)}, f32[16,2,1,8]{0,3,1,2:T(8,128)S(1)}, f32[16,2,1,8]{0,3,1,2:T(8,128)S(1)}, f32[16,2,1,8,128]{4,0,3,1,2:T(8,128)}, bf16[4,1024,1,128]...) while((s32[]{:T(128)}, f32[16,2,1,8]{0,3,1,2:T(8,128)S(1)}, ...), condition=%wide.region_11.12_spmd.clone, body=%wide.region_8.11_spmd.clone.sunk | while | flops 135890432 | bytes 4028529 | solution.py:50
  344.8 1.1 fusion.201
  346.3 0.4 fusion.198
  346.7 2.0 fusion.201
  349.0 0.4 fusion.198
  349.4 2.0 fusion.201
  352.1 2.0 fusion.201
  354.5 78.2 %collective-permute-done.3 = bf16[1,4096,2,1,128]{4,1,2,3,0:T(8,128)(2,1)} collective-permute-done((bf16[1,4096,2,1,128]{4,1,2,3,0:T(8,128)(2,1)}, bf16[1,4096,2,1,128]{4,1,2,3,0:T(8,128)(2,1)}, u32[]{:S(2)}, u32[]{:S(2)}) %collective-permute-start.3) | collective-permute-done | bytes 2097184 | tf_op jit(solution)/shard_map/ppermute | solution.py:11
  432.6 1.7 fusion.141
  434.3 10.0 %while.93 = (s32[]{:T(128)}, f32[16,2,1,8]{0,3,1,2:T(8,128)S(1)}, f32[16,2,1,8]{0,3,1,2:T(8,128)S(1)}, f32[16,2,1,8,128]{4,0,3,1,2:T(8,128)}, bf16[4,1024,1,128]...) while((s32[]{:T(128)}, f32[16,2,1,8]{0,3,1,2:T(8,128)S(1)}, ...), condition=%wide.region_15.16_spmd.clone, body=%wide.region_12.15_spmd.clone.sunk | while | flops 135890432 | bytes 4028529 | solution.py:50
  434.7 1.1 fusion.207
  436.6 2.0 fusion.207
  439.3 2.0 fusion.207
  442.0 2.0 fusion.207
  444.4 84.0 %collective-permute-done.4 = bf16[1,4096,2,1,128]{4,1,2,3,0:T(8,128)(2,1)} collective-permute-done((bf16[1,4096,2,1,128]{4,1,2,3,0:T(8,128)(2,1)}, bf16[1,4096,2,1,128]{4,1,2,3,0:T(8,128)(2,1)}, u32[]{:S(2)}, u32[]{:S(2)}) %collective-permute-start.4) | collective-permute-done | bytes 2097184 | tf_op jit(solution)/shard_map/ppermute | solution.py:11
  528.4 1.7 fusion.142
  530.1 10.1 %while.94 = (s32[]{:T(128)}, f32[16,2,1,8]{0,3,1,2:T(8,128)S(1)}, f32[16,2,1,8]{0,3,1,2:T(8,128)S(1)}, f32[16,2,1,8,128]{4,0,3,1,2:T(8,128)}, bf16[4,1024,1,128]...) while((s32[]{:T(128)}, f32[16,2,1,8]{0,3,1,2:T(8,128)S(1)}, ...), condition=%wide.region_19.20_spmd.clone, body=%wide.region_16.19_spmd.clone.sunk | while | flops 135890432 | bytes 4028529 | solution.py:50
  530.5 1.1 fusion.213
  532.3 2.0 fusion.213
  534.7 0.4 fusion.210
  535.1 2.0 fusion.213
  537.8 2.0 fusion.213
  540.2 79.2 %collective-permute-done.5 = bf16[1,4096,2,1,128]{4,1,2,3,0:T(8,128)(2,1)} collective-permute-done((bf16[1,4096,2,1,128]{4,1,2,3,0:T(8,128)(2,1)}, bf16[1,4096,2,1,128]{4,1,2,3,0:T(8,128)(2,1)}, u32[]{:S(2)}, u32[]{:S(2)}) %collective-permute-start.5) | collective-permute-done | bytes 2097184 | tf_op jit(solution)/shard_map/ppermute | solution.py:11
  619.3 1.7 fusion.143
  621.0 4.8 while.95
  621.0 0.4 fusion.216
  621.4 0.4 fusion.219
  622.6 0.4 fusion.219
  623.8 0.4 fusion.219
  625.0 0.4 fusion.219
  626.3 1.2 fusion.101
  627.8 2.0 fusion.98
  629.8 0.7 reshape.382
  (168 shorter events, 16.4 us)
Async XLA Ops:
  0.0 69.9 %copy-start = (s32[64]{0:T(128)S(1)}, s32[64]{0:T(128)}, u32[]{:S(2)}) copy-start(s32[64]{0:T(128)} %param.23) | copy-start | bytes 772
  59.5 6.6 %copy-start.3 = (bf16[16,2,1024]{2,1,0:T(2,128)(2,1)S(1)}, bf16[16,2,1024]{2,1,0:T(2,128)(2,1)}, u32[]{:S(2)}) copy-start(bf16[16,2,1024]{2,1,0:T(2,128)(2,1)} %param.19) | copy-start | bytes 196612
  59.5 6.7 %copy-start.1 = (bf16[16,256,2,128]{3,2,1,0:T(2,128)(2,1)S(1)}, bf16[16,256,2,128]{3,2,1,0:T(2,128)(2,1)}, u32[]{:S(2)}) copy-start(bf16[16,256,2,128]{3,2,1,0:T(2,128)(2,1)} %param.21) | copy-start | bytes 6291460
  61.0 104.6 %collective-permute-start = (bf16[1,4096,2,1,128]{4,1,2,3,0:T(8,128)(2,1)}, bf16[1,4096,2,1,128]{4,1,2,3,0:T(8,128)(2,1)}, u32[]{:S(2)}, u32[]{:S(2)}) collective-permute-start(bf16[1,4096,2,1,128]{4,1,2,3,0:T(8,128)(2,1)} %bitcast.2), channel_id=1, source_target_pairs={{0,48},{8,56},{16,64},{24,72},{32,80},{40,88},{48,96},{56,104},{64... | collective-permute-start | bytes 6291464 | tf_op jit(solution)/shard_map/ppermute | solution.py:11
  66.2 0.7 copy-start.5
  66.3 3.1 copy-start.4
  66.3 3.6 copy-start.6
  66.9 1.3 copy-start.2
  70.6 184.1 %collective-permute-start.1 = (bf16[1,4096,2,1,128]{4,1,2,3,0:T(8,128)(2,1)}, bf16[1,4096,2,1,128]{4,1,2,3,0:T(8,128)(2,1)}, u32[]{:S(2)}, u32[]{:S(2)}) collective-permute-start(bf16[1,4096,2,1,128]{4,1,2,3,0:T(8,128)(2,1)} %bitcast.2), channel_id=1, source_target_pairs={{0,40},{8,48},{16,56},{24,64},{32,72},{40,80},{48,88},{56,96},{64,... | collective-permute-start | bytes 6291464 | tf_op jit(solution)/shard_map/ppermute | solution.py:11
  73.9 268.9 %collective-permute-start.2 = (bf16[1,4096,2,1,128]{4,1,2,3,0:T(8,128)(2,1)}, bf16[1,4096,2,1,128]{4,1,2,3,0:T(8,128)(2,1)}, u32[]{:S(2)}, u32[]{:S(2)}) collective-permute-start(bf16[1,4096,2,1,128]{4,1,2,3,0:T(8,128)(2,1)} %bitcast.2), channel_id=1, source_target_pairs={{0,32},{8,40},{16,48},{24,56},{32,64},{40,72},{48,80},{56,88},{64,... | collective-permute-start | bytes 6291464 | tf_op jit(solution)/shard_map/ppermute | solution.py:11
  77.1 355.6 %collective-permute-start.3 = (bf16[1,4096,2,1,128]{4,1,2,3,0:T(8,128)(2,1)}, bf16[1,4096,2,1,128]{4,1,2,3,0:T(8,128)(2,1)}, u32[]{:S(2)}, u32[]{:S(2)}) collective-permute-start(bf16[1,4096,2,1,128]{4,1,2,3,0:T(8,128)(2,1)} %bitcast.2), channel_id=1, source_target_pairs={{0,24},{8,32},{16,40},{24,48},{32,56},{40,64},{48,72},{56,80},{64,... | collective-permute-start | bytes 6291464 | tf_op jit(solution)/shard_map/ppermute | solution.py:11
  83.6 444.8 %collective-permute-start.4 = (bf16[1,4096,2,1,128]{4,1,2,3,0:T(8,128)(2,1)}, bf16[1,4096,2,1,128]{4,1,2,3,0:T(8,128)(2,1)}, u32[]{:S(2)}, u32[]{:S(2)}) collective-permute-start(bf16[1,4096,2,1,128]{4,1,2,3,0:T(8,128)(2,1)} %bitcast.2), channel_id=1, source_target_pairs={{0,16},{8,24},{16,32},{24,40},{32,48},{40,56},{48,64},{56,72},{64,... | collective-permute-start | bytes 6291464 | tf_op jit(solution)/shard_map/ppermute | solution.py:11
  165.6 453.8 %collective-permute-start.5 = (bf16[1,4096,2,1,128]{4,1,2,3,0:T(8,128)(2,1)}, bf16[1,4096,2,1,128]{4,1,2,3,0:T(8,128)(2,1)}, u32[]{:S(2)}, u32[]{:S(2)}) collective-permute-start(bf16[1,4096,2,1,128]{4,1,2,3,0:T(8,128)(2,1)} %bitcast.2), channel_id=1, source_target_pairs={{0,8},{8,16},{16,24},{24,32},{32,40},{40,48},{48,56},{56,64},{64,7... | collective-permute-start | bytes 6291464 | tf_op jit(solution)/shard_map/ppermute | solution.py:11
where the time goes:
time: 631 us; the launch traced here: 630 us
  waiting for transfers between devices  471 us (75%)
  blocking collectives  57.3 us (9%)
  matrix products  49.5 us (8%)
  starting transfers between devices  23.8 us (4%)
  local copies, waits for them, and re-layouts  17.7 us (3%)
  other arithmetic  9.21 us (1%)
    ppermute x6, waiting for transfers between devices, passed_along(): return lax.ppermute(x, axis, [(i, (i + by) % peers) for i in range(peers)])  471 us
    all_to_all x1, blocking collectives, on_device(): lax.all_to_all(prefix_kv, 'tensor', split_axis=3, concat_axis=1, tiled=True)  57.3 us
    dot_general x24, matrix products, advance(): jnp.einsum('rtkjp,pkd->rtkjd', weights.astype(jnp.bfloat16), block_pair[1...  36.7 us
    ppermute x6, starting transfers between devices, passed_along(): return lax.ppermute(x, axis, [(i, (i + by) % peers) for i in range(peers)])  23.8 us
  transfers between devices with their start and end apart: 6, of which 6 were waited for; matrix products, arithmetic and copies ran while one was open for 10% of the time, Pallas kernels for 0%

commit v1 on v0

v1 whole, which is shorter than its diff:
```python
import functools

import jax
import jax.numpy as jnp
from jax import lax
from jax.experimental import pallas as pl
from jax.experimental.pallas import tpu as pltpu
from jax.sharding import PartitionSpec as P

WINDOW = 8
DRAFT = 2
BLOCK_ROWS = 16
FENCE_FLOPS = 20_000_000_000
VMEM_BYTES = 48 * 1024 * 1024


def nt_dot(left, right):
    return lax.dot_general(left, right, (((1,), (1,)), ((), ())), preferred_element_type=jnp.float32)


def local_kernel(len_ref, q_ref, kv_ref, out_ref, lse_ref):
    rows, vectors, head_dim = q_ref.shape
    slots = kv_ref.shape[2]
    cached = slots - 16
    scaling = head_dim ** (-0.5)
    place = lax.broadcasted_iota(jnp.int32, (vectors, slots), 1)
    token = lax.broadcasted_iota(jnp.int32, (vectors, slots), 0) // (vectors // DRAFT)
    fresh = (place >= cached) & (place - cached <= token)
    for row in range(rows):
        scores = nt_dot(q_ref[row], kv_ref[row, 0]) * scaling
        live = (place < jnp.minimum(len_ref[row], cached)) | fresh
        scores = jnp.where(live, scores, -jnp.inf)
        maxima = scores.max(-1, keepdims=True)
        weights = jnp.exp(scores - maxima)
        totals = weights.sum(-1, keepdims=True)
        summed = jnp.dot(
            weights.astype(jnp.bfloat16), kv_ref[row, 1], preferred_element_type=jnp.float32
        )
        out_ref[row] = summed / totals
        lse_ref[row] = jnp.broadcast_to(maxima + jnp.log(totals), (vectors, head_dim))


def local_attention(queries, own_kv, new_kv, own_len):
    rows, vectors, head_dim = queries.shape
    cache = jnp.concatenate([own_kv, new_kv], axis=1)
    cache = jnp.pad(cache, ((0, 0), (0, 16 - DRAFT), (0, 0), (0, 0)))
    cache = cache.transpose(0, 2, 1, 3)
    shape = jax.ShapeDtypeStruct((rows, vectors, head_dim), jnp.float32)
    vmem = pl.BlockSpec(memory_space=pltpu.VMEM)
    return pl.pallas_call(
        local_kernel,
        out_shape=(shape, shape),
        in_specs=[pl.BlockSpec(memory_space=pltpu.SMEM), vmem, vmem],
        out_specs=(vmem, vmem),
        compiler_params=pltpu.CompilerParams(vmem_limit_bytes=VMEM_BYTES),
        cost_estimate=pl.CostEstimate(flops=300_000_000, bytes_accessed=2_500_000, transcendentals=70_000),
        name="local_attention",
    )(own_len, queries, cache)


def prefix_kernel(live_ref, q_ref, *rest):
    *kv_refs, out_ref, packed, scores, stats, index = rest
    cells, heads, tiles, vectors, head_dim = q_ref.shape
    rows = tiles - 1
    chunk = kv_refs[0].shape[2]
    width = BLOCK_ROWS * vectors
    scaling = head_dim ** (-0.5)

    out_ref[...] = jnp.zeros_like(out_ref)
    stats[...] = jnp.zeros_like(stats)
    packed[...] = jnp.zeros_like(packed)

    def pack(slot, count):
        cell, row = slot // rows, slot % rows
        for head in range(heads):
            packed[head, count] = q_ref[cell, head, row]
        index[count] = slot
        return count + live_ref[slot]

    count = lax.fori_loop(0, cells * rows, pack, jnp.int32(0), unroll=4)

    lane = lax.broadcasted_iota(jnp.int32, (vectors, head_dim), 1)
    vector = lax.broadcasted_iota(jnp.int32, (vectors, head_dim), 0)
    on_lane = (lane % vectors == vector) & (lane < 3 * vectors)
    piece = lane // vectors

    def block(step, carry):
        first = step * BLOCK_ROWS
        for head in range(heads):
            q = packed[head, pl.ds(first, BLOCK_ROWS)].reshape(width, head_dim)
            maxima = None
            for part, kv in enumerate(kv_refs):
                product = nt_dot(q, kv[head, 0]) * scaling
                scores[part] = product
                top = product.max(-1, keepdims=True)
                maxima = top if maxima is None else jnp.maximum(maxima, top)
            totals = jnp.zeros((width, 1), jnp.float32)
            summed = jnp.zeros((width, head_dim), jnp.float32)
            for part, kv in enumerate(kv_refs):
                weights = jnp.exp(scores[part] - maxima)
                totals = totals + weights.sum(-1, keepdims=True)
                summed = summed + jnp.dot(
                    weights.astype(jnp.bfloat16), kv[head, 1], preferred_element_type=jnp.float32
                )
            attended = (summed / totals).astype(jnp.bfloat16)
            level = jnp.broadcast_to(maxima + jnp.log(totals), (width, head_dim))
            high = level.astype(jnp.bfloat16).astype(jnp.float32)
            middle = (level - high).astype(jnp.bfloat16).astype(jnp.float32)
            low = level - high - middle
            for row in range(BLOCK_ROWS):
                span = slice(row * vectors, (row + 1) * vectors)
                pieces = jnp.where(piece == 0, high[span], jnp.where(piece == 1, middle[span], low[span]))
                line = jnp.where(on_lane, pieces, 0.0).sum(0, keepdims=True)

                @pl.when(first + row < count)
                def _(row=row, span=span, line=line):
                    slot = index[first + row]
                    out_ref[slot // rows, head, slot % rows] = attended[span]
                    stats[head, pl.ds(slot, 1), :] = line

        return carry

    lax.fori_loop(0, (count + BLOCK_ROWS - 1) // BLOCK_ROWS, block, 0)
    for cell in range(cells):
        for head in range(heads):
            out_ref[cell, head, rows] = stats[head, cell * rows : (cell + 1) * rows, :].astype(jnp.bfloat16)


def prefix_attention(live, arrived, blocks):
    cells, heads, tiles, vectors, head_dim = arrived.shape
    slots = cells * (tiles - 1)
    chunk = blocks[0].shape[2]
    vmem = pl.BlockSpec(memory_space=pltpu.VMEM)
    return pl.pallas_call(
        prefix_kernel,
        out_shape=jax.ShapeDtypeStruct(arrived.shape, jnp.bfloat16),
        in_specs=[pl.BlockSpec(memory_space=pltpu.SMEM)] + [vmem] * (1 + len(blocks)),
        out_specs=vmem,
        scratch_shapes=[
            pltpu.VMEM((heads, slots + BLOCK_ROWS, vectors, head_dim), jnp.bfloat16),
            pltpu.VMEM((len(blocks), BLOCK_ROWS * vectors, chunk), jnp.float32),
            pltpu.VMEM((heads, slots, head_dim), jnp.float32),
            pltpu.SMEM((slots + 1,), jnp.int32),
        ],
        compiler_params=pltpu.CompilerParams(vmem_limit_bytes=VMEM_BYTES),
        cost_estimate=pl.CostEstimate(flops=1_000_000_000, bytes_accessed=4_000_000, transcendentals=2_000_000),
        name="prefix_attention",
    )(live, arrived, *blocks)


def merge_kernel(*refs):
    *part_refs, local_ref, local_lse_ref, out_ref = refs
    rows, vectors, head_dim = local_ref.shape
    lane = lax.broadcasted_iota(jnp.int32, (vectors, head_dim), 1)
    vector = lax.broadcasted_iota(jnp.int32, (vectors, head_dim), 0)
    on_lane = (lane % vectors == vector) & (lane < 3 * vectors)
    pairs = [part_refs[k : k + 2] for k in range(0, len(part_refs), 2)]
    levels = [one[rows].astype(jnp.float32) + other[rows].astype(jnp.float32) for one, other in pairs]
    for row in range(rows):
        terms = [(local_ref[row], local_lse_ref[row])]
        for (one, other), level in zip(pairs, levels):
            line = jnp.broadcast_to(level[row : row + 1], (vectors, head_dim))
            lse = jnp.where(on_lane, line, 0.0).sum(-1, keepdims=True)
            attended = one[row].astype(jnp.float32) + other[row].astype(jnp.float32)
            terms.append((attended, jnp.broadcast_to(lse, (vectors, head_dim))))
        maxima = functools.reduce(jnp.maximum, [lse for _, lse in terms])
        scales = [jnp.exp(lse - maxima) for _, lse in terms]
        summed = sum(scale * term for scale, (term, _) in zip(scales, terms))
        out_ref[row] = (summed / sum(scales)).astype(jnp.bfloat16)


def merge_parts(parts, local, local_lse):
    vmem = pl.BlockSpec(memory_space=pltpu.VMEM)
    return pl.pallas_call(
        merge_kernel,
        out_shape=jax.ShapeDtypeStruct(local.shape, jnp.bfloat16),
        in_specs=[vmem] * (len(parts) + 2),
        out_specs=vmem,
        compiler_params=pltpu.CompilerParams(vmem_limit_bytes=VMEM_BYTES),
        name="merge_parts",
    )(*parts, local, local_lse)


def split_kernel(lane_ref, prefix_ref, *rest):
    *out_refs, by_head = rest
    positions, sides, heads, head_dim = prefix_ref.shape
    quad = len(out_refs)
    for side in range(sides):
        by_head[side] = jnp.swapaxes(prefix_ref[:, side], 0, 1)
    for step, out_ref in enumerate(out_refs):
        first = lane_ref[0] ^ step
        for half in range(heads // quad):
            for side in range(sides):
                out_ref[half, side] = by_head[side, first + half * quad]


def split_prefix(lane, prefix):
    positions, sides, heads, head_dim = prefix.shape
    quad = heads // 2
    shape = jax.ShapeDtypeStruct((2, sides, positions, head_dim), prefix.dtype)
    vmem = pl.BlockSpec(memory_space=pltpu.VMEM)
    return pl.pallas_call(
        split_kernel,
        out_shape=[shape] * quad,
        in_specs=[pl.BlockSpec(memory_space=pltpu.SMEM), vmem],
        out_specs=[vmem] * quad,
        scratch_shapes=[pltpu.VMEM((sides, heads, positions, head_dim), prefix.dtype)],
        compiler_params=pltpu.CompilerParams(vmem_limit_bytes=VMEM_BYTES),
        cost_estimate=pl.CostEstimate(flops=0, bytes_accessed=4 * 1024 * 1024, transcendentals=0),
        name="split_prefix",
    )(lane.reshape(1), prefix)


def fence_kernel(*refs):
    del refs


def fence(arrays):
    place = pl.BlockSpec(memory_space=pl.ANY)
    return pl.pallas_call(
        fence_kernel,
        out_shape=[jax.ShapeDtypeStruct(x.shape, x.dtype) for x in arrays],
        in_specs=[place] * len(arrays),
        out_specs=[place] * len(arrays),
        input_output_aliases={k: k for k in range(len(arrays))},
        cost_estimate=pl.CostEstimate(flops=FENCE_FLOPS, bytes_accessed=0, transcendentals=0),
        name="fence",
    )(*arrays)


def moved(x, by, flip=0):
    groups, lanes = lax.axis_size("group"), lax.axis_size("tensor")
    pairs = [
        (g * lanes + t, (g + by) % groups * lanes + (t ^ flip)) for g in range(groups) for t in range(lanes)
    ]
    return lax.ppermute(x, ("group", "tensor"), pairs)


def windowed(x):
    groups = lax.axis_size("group")
    windows = [list(range(first, first + WINDOW)) for first in range(0, groups, WINDOW)]
    return lax.all_to_all(x, "group", 0, 0, axis_index_groups=windows, tiled=True)


def on_device(queries, new_kv, own_kv, prefix_kv, owner, parent, own_len):
    rows, draft, width = queries.shape
    head_dim = prefix_kv.shape[4]
    per_kv = width // head_dim
    vectors = draft * per_kv
    me = lax.axis_index("group")
    lane = lax.axis_index("tensor")
    place = me % WINDOW
    cells = jnp.arange(WINDOW)

    distance = (me - owner[parent]) % lax.axis_size("group")
    tag = jnp.broadcast_to(distance.astype(jnp.bfloat16)[None, :, None], (1, rows, head_dim))
    q = queries.reshape(rows, vectors, head_dim)
    sent = jnp.concatenate([q, tag.reshape(1, vectors, head_dim)])
    quad = prefix_kv.shape[3] // 2
    partner = moved(sent, 0, quad)
    blocks = split_prefix(lane % quad, prefix_kv[0])
    *blocks, partner = lax.optimization_barrier([*blocks, partner])
    blocks = blocks[:1] + list(fence([moved(blocks[step], 0, step) for step in range(1, quad)]))
    upper = lane >= quad

    def both(own, other):
        return jnp.where(upper, jnp.stack([other, own]), jnp.stack([own, other]))

    here = both(sent, partner)
    after = moved(here, -WINDOW)
    mine = (cells < place)[:, None, None, None, None]
    arrived = windowed(jnp.where(mine, here, after))
    tags = arrived[:, 0, rows, :, 0].astype(jnp.int32)
    live = (tags > 0) & (tags == ((cells - place) % WINDOW)[:, None])
    local, local_lse = local_attention(q, own_kv, new_kv, own_len)
    arrived, local, local_lse = lax.optimization_barrier((arrived, local, local_lse))
    partial = prefix_attention(live.reshape(-1).astype(jnp.int32), arrived, blocks)

    returned = windowed(partial)
    here = jnp.where(mine, returned, 0).sum(0)
    after = jnp.where(mine, 0, returned).sum(0)
    here_own, here_other = jnp.where(upper, here[1], here[0]), jnp.where(upper, here[0], here[1])
    after_own, after_other = jnp.where(upper, after[1], after[0]), jnp.where(upper, after[0], after[1])
    parts = [here_own, moved(after_own, WINDOW), moved(here_other, 0, quad), moved(after_other, WINDOW, quad)]
    return merge_parts(parts, local, local_lse).reshape(rows, draft, width)


def solution(mesh):
    placed = (
        P("group", None, "tensor"),
        P("group", None, None, "tensor"),
        P("group", None, None, "tensor"),
        P("group", "tensor", None, None, None),
        P(),
        P("group"),
        P("group"),
    )
    return jax.shard_map(
        on_device, mesh=mesh, in_specs=placed, out_specs=P("group", None, "tensor"), check_vma=False
    )
```

time: 631 us -> 107 us (0.17)
  waiting for transfers between devices: 471 us -> 19.7 us
  matrix products: 49.5 us -> 0 us
  blocking collectives: 57.3 us -> 24.9 us
  starting transfers between devices: 23.8 us -> 37.9 us
  Pallas kernels: 0 us -> 12.1 us
  local copies, waits for them, and re-layouts: 17.7 us -> 8.32 us
  other arithmetic: 9.21 us -> 2.81 us
    ppermute x6 -> x8, waiting for transfers between devices: 471 us -> 19.7 us  [moved(): return lax.ppermute(x, ('group', 'tensor'), pairs)]
    dot_general x52 -> x0, matrix products: 49.5 us -> none  [the longest x24 36.7 us: advance(): jnp.einsum('rtkjp,pkd->rtkjd', weights.astype(jnp.bfloat16), block_pair[1...]
    all_to_all x1, blocking collectives: 57.3 us -> 24.9 us  [windowed(): lax.all_to_all(x, 'group', 0, 0, axis_index_groups=windows, tiled=True)]
    pallas_call x0 -> x5, Pallas kernels: none -> 12.1 us  [the longest x1 5.37 us: prefix_attention(): pl.pallas_call(prefix_kernel, out_shape=jax.ShapeDtypeStruct(arrived.shap...]
    slice x6 -> x0, local copies, waits for them, and re-layouts: 10.1 us -> none  [on_device(): partial_terms = prefix_partial(grouped, arrived[0, :, 0], arrived[0, :, 1])]
    ppermute x6 -> x8, starting transfers between devices: 23.8 us -> 33.8 us  [moved(): return lax.ppermute(x, ('group', 'tensor'), pairs)]
    reduce_sum x26 -> x1, other arithmetic: 8.49 us -> 0.46 us  [on_device(): after = jnp.where(mine, 0, returned).sum(0)]
  transfers between devices with their start and end apart: 6 -> 9, of which waited for: 6 -> 3; matrix products, arithmetic and copies ran while one was open for 10% -> 6% of each run, Pallas kernels for 0% -> 6%
where the time goes in v1:
time: 107 us; the launch traced here: 106 us
  starting transfers between devices  37.9 us (35%)
  blocking collectives  24.9 us (23%)
  waiting for transfers between devices  19.7 us (18%)
  Pallas kernels  12.1 us (11%)
  local copies, waits for them, and re-layouts  8.32 us (8%)
  other arithmetic  2.81 us (3%)
    ppermute x8, starting transfers between devices, moved(): return lax.ppermute(x, ('group', 'tensor'), pairs)  33.8 us
    all_to_all x1, blocking collectives, windowed(): lax.all_to_all(x, 'group', 0, 0, axis_index_groups=windows, tiled=True)  24.9 us
    ppermute x8, waiting for transfers between devices, moved(): return lax.ppermute(x, ('group', 'tensor'), pairs)  19.7 us
    unnamed x18, local copies, waits for them, and re-layouts  5.81 us
    pallas_call x1, Pallas kernels, prefix_attention(): pl.pallas_call(prefix_kernel, out_shape=jax.ShapeDtypeStruct(arrived.shap...  5.37 us
    pallas_call x1, Pallas kernels, local_attention(): pl.pallas_call(local_kernel, out_shape=(shape, shape), in_specs=[pl.Block...  4.53 us
    all_to_all x1, starting transfers between devices, windowed(): lax.all_to_all(x, 'group', 0, 0, axis_index_groups=windows, tiled=True)  4.13 us
  transfers between devices with their start and end apart: 9, of which 3 were waited for; matrix products, arithmetic and copies ran while one was open for 6% of the time, Pallas kernels for 6%

profile of v1, /device:TPU:1, one launch (start us, length us, event | category | flops | bytes accessed | tf_op | source)
XLA Modules:
  0.0 106.0 jit_solution(14778340829570084635)
XLA Ops:
  0.0 0.0 copy-start
  0.0 0.7 compare_select_fusion
  0.7 0.9 reshape.59.q_ref
  1.6 0.0 copy-done
  1.6 0.7 gather_fusion
  2.3 0.1 broadcast_in_dim.47
  2.4 6.6 %collective-permute-start = (bf16[17,16,128]{2,1,0:T(8,128)(2,1)S(1)}, bf16[17,16,128]{2,1,0:T(8,128)(2,1)S(1)}, u32[]{:S(2)}, u32[]{:S(2)}) collective-permute-start(bf16[17,16,128]{2,1,0:T(8,128)(2,1)S(1)} %get-tuple-element.45), channel_id=1, source_target_pairs={{0,4},{1,5},{2,6},{3,7},{4,0},{5,1},{6,2},{7,3},{8,12},{9,13},{10,... | collective-permute-start | bytes 208904 | tf_op jit(solution)/shard_map/ppermute | solution.py:236
  9.0 0.7 copy.14
  9.7 0.0 copy-start.1
  9.8 3.6 %copy.13 = bf16[16,256,2,128]{3,1,2,0:T(8,128)(2,1)} copy(bf16[16,256,2,128]{3,2,1,0:T(2,128)(2,1)} %param.9) | data formatting | bytes 4194304 | tf_op args[2]
  13.3 0.0 copy-start.7
  13.3 0.0 copy-done.1
  13.3 2.0 %split_prefix.1 = (bf16[2,2,512,128]{3,2,1,0:T(8,128)(2,1)S(1)}, bf16[2,2,512,128]{3,2,1,0:T(8,128)(2,1)}, bf16[2,2,512,128]{3,2,1,0:T(8,128)(2,1)}, bf16[2,2,512,128]{3,2,1,0:T(8,128)(2,1)}) custom-call(s32[1]{0:T(128)} %bitcast.lane_ref, bf16[512,2,8,128]{3,2,1,0:T(8,128)(2,1)S(1)} %bitcast.15), custom_call_target="tpu_custom_call" | custom-call | bytes 4194304 | tf_op jit(solution)/shard_map/split_prefix/pallas_call | solution.py:202
  15.4 0.0 copy-start.2
  15.4 0.8 copy-done.2
  16.2 0.0 collective-permute-done
  16.2 12.5 %collective-permute-start.1 = (bf16[2,17,16,128]{3,2,1,0:T(8,128)(2,1)S(1)}, bf16[2,17,16,128]{3,2,1,0:T(8,128)(2,1)S(1)}, u32[]{:S(2)}, u32[]{:S(2)}) collective-permute-start(bf16[2,17,16,128]{3,2,1,0:T(8,128)(2,1)S(1)} %maximum_select_fusion), channel_id=1, source_target_pairs={{0,448},{1,449},{2,450},{3,451},{4,452},{5,453},{6,454},{7,455},{8... | collective-permute-start | bytes 417800 | tf_op jit(solution)/shard_map/ppermute | solution.py:236
  28.7 3.1 %collective-permute-start.2 = (bf16[2,2,512,128]{3,2,1,0:T(8,128)(2,1)}, bf16[2,2,512,128]{3,2,1,0:T(8,128)(2,1)}, u32[]{:S(2)}, u32[]{:S(2)}) collective-permute-start(bf16[2,2,512,128]{3,2,1,0:T(8,128)(2,1)} %get-tuple-element.31), channel_id=1, source_target_pairs={{0,1},{1,0},{2,3},{3,2},{4,5},{5,4},{6,7},{7,6},{8,9},{9,8},{10,11... | collective-permute-start | bytes 1572872 | tf_op jit(solution)/shard_map/ppermute | solution.py:236
  31.9 3.1 %collective-permute-start.3 = (bf16[2,2,512,128]{3,2,1,0:T(8,128)(2,1)}, bf16[2,2,512,128]{3,2,1,0:T(8,128)(2,1)}, u32[]{:S(2)}, u32[]{:S(2)}) collective-permute-start(bf16[2,2,512,128]{3,2,1,0:T(8,128)(2,1)} %get-tuple-element.32), channel_id=1, source_target_pairs={{0,2},{1,3},{2,0},{3,1},{4,6},{5,7},{6,4},{7,5},{8,10},{9,11},{10,... | collective-permute-start | bytes 1572872 | tf_op jit(solution)/shard_map/ppermute | solution.py:236
  35.0 2.4 %collective-permute-start.4 = (bf16[2,2,512,128]{3,2,1,0:T(8,128)(2,1)}, bf16[2,2,512,128]{3,2,1,0:T(8,128)(2,1)}, u32[]{:S(2)}, u32[]{:S(2)}) collective-permute-start(bf16[2,2,512,128]{3,2,1,0:T(8,128)(2,1)} %get-tuple-element.33), channel_id=1, source_target_pairs={{0,3},{1,2},{2,1},{3,0},{4,7},{5,6},{6,5},{7,4},{8,11},{9,10},{10,... | collective-permute-start | bytes 1572872 | tf_op jit(solution)/shard_map/ppermute | solution.py:236
  37.4 0.0 copy-done.7
  37.4 0.2 fusion.3.kv_ref
  37.6 0.0 copy-start.6
  37.6 0.0 collective-permute-done.1
  37.6 1.2 %broadcast_select_fusion = bf16[8,2,17,16,128]{4,3,2,1,0:T(8,128)(2,1)} fusion(pred[8]{0:T(512)(128)(4,1)S(1)} %iota_compare_fusion.1, bf16[2,17,16,128]{3,2,1,0:T(8,128)(2,1)S(1)} %collective-permute-done.1, bf16[2,17,16,128]{3,2,1,0:T(8,128)(2,1)S(1)} %maximum_select_fusion), kind=kLoop, calls=%fused_computation.8 | loop fusion | flops 557056 | bytes 1392648 | tf_op jit(solution)/shard_map/jit(_where)/select_n | solution.py:272
  38.8 4.1 %all-to-all-start = ((bf16[8,2,17,16,128]{4,3,2,1,0:T(8,128)(2,1)}), bf16[8,2,17,16,128]{4,3,2,1,0:T(8,128)(2,1)S(1)}, u32[]{:S(2)}, u32[]{:S(2)}) async-start(bf16[8,2,17,16,128]{4,3,2,1,0:T(8,128)(2,1)} %broadcast_select_fusion), calls=%async_computation | async-start | bytes 2228224 | tf_op jit(solution)/shard_map/all_to_all | solution.py:242
  42.9 0.1 eq.18
  43.0 0.1 eq.19
  43.1 0.0 copy-done.6
  43.1 4.5 %local_attention.1 = (f32[16,16,128]{2,1,0:T(8,128)S(1)}, f32[16,16,128]{2,1,0:T(8,128)S(1)}) custom-call(s32[16]{0:T(128)S(1)} %copy-done.6, bf16[16,16,128]{2,1,0:T(8,128)(2,1)S(1)} %reshape.59.q_ref, bf16[16,2,272,128]{3,2,1,0:T(8,128)(2,1)S(1)} %fusion.3.kv_ref), custom_call_target="tpu_custom_call" | custom-call | flops 300000000 | bytes 2500000 | tf_op jit(solution)/shard_map/local_attention/pallas_call | solution.py:50
  47.6 0.0 copy-start.4
  47.6 0.7 copy-done.4
  48.3 0.0 copy-start.3
  48.3 0.0 collective-permute-done.2.refs_0_
  48.3 0.0 collective-permute-done.3.refs_1_
  48.3 10.7 %collective-permute-done.4.refs_2_ = bf16[2,2,512,128]{3,2,1,0:T(8,128)(2,1)} collective-permute-done((bf16[2,2,512,128]{3,2,1,0:T(8,128)(2,1)}, bf16[2,2,512,128]{3,2,1,0:T(8,128)(2,1)}, u32[]{:S(2)}, u32[]{:S(2)}) %collective-permute-start.4) | collective-permute-done | bytes 524320 | tf_op jit(solution)/shard_map/ppermute | solution.py:236
  59.0 0.0 all-to-all-done.q_ref
  59.0 0.2 convert_reduce_fusion
  59.2 0.1 reshape.61
  59.3 0.0 copy-done.3
  59.3 5.4 %prefix_attention.1 = bf16[8,2,17,16,128]{4,3,2,1,0:T(8,128)(2,1)S(1)} custom-call(s32[128]{0:T(128)S(1)} %and_convert_fusion.live_ref, bf16[8,2,17,16,128]{4,3,2,1,0:T(8,128)(2,1)S(1)} %all-to-all-done.q_ref, bf16[2,2,512,128]{3,2,1,0:T(8,128)(2,1)S(1)} %copy-done.3, bf16[2,2,512,128]{3,2,1,0:T(8,128)(2,1)} %get-tuple-element.34.rest_1_, ...), custom_call_target="tpu_custom_call" | custom-call | flops 1000000000 | bytes 4000000 | tf_op jit(solution)/shard_map/prefix_attention/pallas_call | solution.py:134
  64.7 0.0 copy-start.5
  64.7 24.9 %all_to_all.10 = bf16[8,2,17,16,128]{4,3,2,1,0:T(8,128)(2,1)S(1)} all-to-all(bf16[8,2,17,16,128]{4,3,2,1,0:T(8,128)(2,1)S(1)} %prefix_attention.1), channel_id=1, replica_groups={{0,8,16,24,32,40,48,56},{64,72,80,88,96,104,112,120},{128,136,144,152,1..., dimensions={0} | all-to-all | bytes 2228224 | tf_op jit(solution)/shard_map/all_to_all | solution.py:242
  89.6 0.5 select_reduce_fusion
  90.1 1.9 %collective-permute-start.7 = (bf16[17,16,128]{2,1,0:T(8,128)(2,1)S(1)}, bf16[17,16,128]{2,1,0:T(8,128)(2,1)S(1)}, u32[]{:S(2)}, u32[]{:S(2)}) collective-permute-start(bf16[17,16,128]{2,1,0:T(8,128)(2,1)S(1)} %get-tuple-element.41), channel_id=1, source_target_pairs={{0,68},{1,69},{2,70},{3,71},{4,64},{5,65},{6,66},{7,67},{8,76},{9,... | collective-permute-start | bytes 208904 | tf_op jit(solution)/shard_map/ppermute | solution.py:236
  92.1 1.9 %collective-permute-start.5 = (bf16[17,16,128]{2,1,0:T(8,128)(2,1)S(1)}, bf16[17,16,128]{2,1,0:T(8,128)(2,1)S(1)}, u32[]{:S(2)}, u32[]{:S(2)}) collective-permute-start(bf16[17,16,128]{2,1,0:T(8,128)(2,1)S(1)} %get-tuple-element.42), channel_id=1, source_target_pairs={{0,64},{1,65},{2,66},{3,67},{4,68},{5,69},{6,70},{7,71},{8,72},{9,... | collective-permute-start | bytes 208904 | tf_op jit(solution)/shard_map/ppermute | solution.py:236
  94.0 2.2 %collective-permute-start.6 = (bf16[17,16,128]{2,1,0:T(8,128)(2,1)S(1)}, bf16[17,16,128]{2,1,0:T(8,128)(2,1)S(1)}, u32[]{:S(2)}, u32[]{:S(2)}) collective-permute-start(bf16[17,16,128]{2,1,0:T(8,128)(2,1)S(1)} %get-tuple-element.43), channel_id=1, source_target_pairs={{0,4},{1,5},{2,6},{3,7},{4,0},{5,1},{6,2},{7,3},{8,12},{9,13},{10,... | collective-permute-start | bytes 208904 | tf_op jit(solution)/shard_map/ppermute | solution.py:236
  96.2 5.4 %collective-permute-done.7.refs_3_ = bf16[17,16,128]{2,1,0:T(8,128)(2,1)S(1)} collective-permute-done((bf16[17,16,128]{2,1,0:T(8,128)(2,1)S(1)}, bf16[17,16,128]{2,1,0:T(8,128)(2,1)S(1)}, u32[]{:S(2)}, u32[]{:S(2)}) %collective-permute-start.7) | collective-permute-done | bytes 69664 | tf_op jit(solution)/shard_map/ppermute | solution.py:236
  101.6 3.6 %collective-permute-done.5.refs_1_ = bf16[17,16,128]{2,1,0:T(8,128)(2,1)S(1)} collective-permute-done((bf16[17,16,128]{2,1,0:T(8,128)(2,1)S(1)}, bf16[17,16,128]{2,1,0:T(8,128)(2,1)S(1)}, u32[]{:S(2)}, u32[]{:S(2)}) %collective-permute-start.5) | collective-permute-done | bytes 69664 | tf_op jit(solution)/shard_map/ppermute | solution.py:236
  105.2 0.0 collective-permute-done.6.refs_2_
  105.2 0.0 copy-done.5
  105.2 0.2 merge_parts.1
  105.4 0.7 reshape.60
  (10 shorter events, 0.1 us)
Async XLA Ops:
  0.0 1.6 %copy-start = (s32[64]{0:T(128)S(1)}, s32[64]{0:T(128)}, u32[]{:S(2)}) copy-start(s32[64]{0:T(128)} %param.11) | copy-start | bytes 772
  2.4 13.8 %collective-permute-start = (bf16[17,16,128]{2,1,0:T(8,128)(2,1)S(1)}, bf16[17,16,128]{2,1,0:T(8,128)(2,1)S(1)}, u32[]{:S(2)}, u32[]{:S(2)}) collective-permute-start(bf16[17,16,128]{2,1,0:T(8,128)(2,1)S(1)} %get-tuple-element.45), channel_id=1, source_target_pairs={{0,4},{1,5},{2,6},{3,7},{4,0},{5,1},{6,2},{7,3},{8,12},{9,13},{10,... | collective-permute-start | bytes 208904 | tf_op jit(solution)/shard_map/ppermute | solution.py:236
  9.7 3.6 %copy-start.1 = (bf16[1,512,2,8,128]{4,3,2,1,0:T(8,128)(2,1)S(1)}, bf16[1,512,2,8,128]{4,3,2,1,0:T(8,128)(2,1)}, u32[]{:S(2)}) copy-start(bf16[1,512,2,8,128]{4,3,2,1,0:T(8,128)(2,1)} %param.10) | copy-start | bytes 6291460
  13.3 24.0 %copy-start.7 = (bf16[16,256,2,128]{3,1,2,0:T(8,128)(2,1)S(1)}, bf16[16,256,2,128]{3,1,2,0:T(8,128)(2,1)}, u32[]{:S(2)}) copy-start(bf16[16,256,2,128]{3,1,2,0:T(8,128)(2,1)} %copy.13) | copy-start | bytes 6291460
  15.4 0.8 copy-start.2
  16.2 21.4 %collective-permute-start.1 = (bf16[2,17,16,128]{3,2,1,0:T(8,128)(2,1)S(1)}, bf16[2,17,16,128]{3,2,1,0:T(8,128)(2,1)S(1)}, u32[]{:S(2)}, u32[]{:S(2)}) collective-permute-start(bf16[2,17,16,128]{3,2,1,0:T(8,128)(2,1)S(1)} %maximum_select_fusion), channel_id=1, source_target_pairs={{0,448},{1,449},{2,450},{3,451},{4,452},{5,453},{6,454},{7,455},{8... | collective-permute-start | bytes 417800 | tf_op jit(solution)/shard_map/ppermute | solution.py:236
  28.7 19.6 %collective-permute-start.2 = (bf16[2,2,512,128]{3,2,1,0:T(8,128)(2,1)}, bf16[2,2,512,128]{3,2,1,0:T(8,128)(2,1)}, u32[]{:S(2)}, u32[]{:S(2)}) collective-permute-start(bf16[2,2,512,128]{3,2,1,0:T(8,128)(2,1)} %get-tuple-element.31), channel_id=1, source_target_pairs={{0,1},{1,0},{2,3},{3,2},{4,5},{5,4},{6,7},{7,6},{8,9},{9,8},{10,11... | collective-permute-start | bytes 1572872 | tf_op jit(solution)/shard_map/ppermute | solution.py:236
  31.9 16.4 %collective-permute-start.3 = (bf16[2,2,512,128]{3,2,1,0:T(8,128)(2,1)}, bf16[2,2,512,128]{3,2,1,0:T(8,128)(2,1)}, u32[]{:S(2)}, u32[]{:S(2)}) collective-permute-start(bf16[2,2,512,128]{3,2,1,0:T(8,128)(2,1)} %get-tuple-element.32), channel_id=1, source_target_pairs={{0,2},{1,3},{2,0},{3,1},{4,6},{5,7},{6,4},{7,5},{8,10},{9,11},{10,... | collective-permute-start | bytes 1572872 | tf_op jit(solution)/shard_map/ppermute | solution.py:236
  35.0 24.0 %collective-permute-start.4 = (bf16[2,2,512,128]{3,2,1,0:T(8,128)(2,1)}, bf16[2,2,512,128]{3,2,1,0:T(8,128)(2,1)}, u32[]{:S(2)}, u32[]{:S(2)}) collective-permute-start(bf16[2,2,512,128]{3,2,1,0:T(8,128)(2,1)} %get-tuple-element.33), channel_id=1, source_target_pairs={{0,3},{1,2},{2,1},{3,0},{4,7},{5,6},{6,5},{7,4},{8,11},{9,10},{10,... | collective-permute-start | bytes 1572872 | tf_op jit(solution)/shard_map/ppermute | solution.py:236
  37.6 5.5 %copy-start.6 = (s32[16]{0:T(128)S(1)}, s32[16]{0:T(128)}, u32[]{:S(2)}) copy-start(s32[16]{0:T(128)} %len_ref.1) | copy-start | bytes 196
  38.8 20.2 %all-to-all-start = ((bf16[8,2,17,16,128]{4,3,2,1,0:T(8,128)(2,1)}), bf16[8,2,17,16,128]{4,3,2,1,0:T(8,128)(2,1)S(1)}, u32[]{:S(2)}, u32[]{:S(2)}) async-start(bf16[8,2,17,16,128]{4,3,2,1,0:T(8,128)(2,1)} %broadcast_select_fusion), calls=%async_computation | async-start | bytes 2228224 | tf_op jit(solution)/shard_map/all_to_all | solution.py:242
  47.6 0.7 copy-start.4
  48.3 11.0 %copy-start.3 = (bf16[2,2,512,128]{3,2,1,0:T(8,128)(2,1)S(1)}, bf16[2,2,512,128]{3,2,1,0:T(8,128)(2,1)}, u32[]{:S(2)}) copy-start(bf16[2,2,512,128]{3,2,1,0:T(8,128)(2,1)} %copy-done.2) | copy-start | bytes 1572868
  64.7 40.5 %copy-start.5 = (f32[16,16,128]{2,1,0:T(8,128)S(1)}, f32[16,16,128]{2,1,0:T(8,128)}, u32[]{:S(2)}) copy-start(f32[16,16,128]{2,1,0:T(8,128)} %copy-done.4) | copy-start | bytes 393220
  90.1 11.4 %collective-permute-start.7 = (bf16[17,16,128]{2,1,0:T(8,128)(2,1)S(1)}, bf16[17,16,128]{2,1,0:T(8,128)(2,1)S(1)}, u32[]{:S(2)}, u32[]{:S(2)}) collective-permute-start(bf16[17,16,128]{2,1,0:T(8,128)(2,1)S(1)} %get-tuple-element.41), channel_id=1, source_target_pairs={{0,68},{1,69},{2,70},{3,71},{4,64},{5,65},{6,66},{7,67},{8,76},{9,... | collective-permute-start | bytes 208904 | tf_op jit(solution)/shard_map/ppermute | solution.py:236
  92.1 13.1 %collective-permute-start.5 = (bf16[17,16,128]{2,1,0:T(8,128)(2,1)S(1)}, bf16[17,16,128]{2,1,0:T(8,128)(2,1)S(1)}, u32[]{:S(2)}, u32[]{:S(2)}) collective-permute-start(bf16[17,16,128]{2,1,0:T(8,128)(2,1)S(1)} %get-tuple-element.42), channel_id=1, source_target_pairs={{0,64},{1,65},{2,66},{3,67},{4,68},{5,69},{6,70},{7,71},{8,72},{9,... | collective-permute-start | bytes 208904 | tf_op jit(solution)/shard_map/ppermute | solution.py:236
  94.0 11.2 %collective-permute-start.6 = (bf16[17,16,128]{2,1,0:T(8,128)(2,1)S(1)}, bf16[17,16,128]{2,1,0:T(8,128)(2,1)S(1)}, u32[]{:S(2)}, u32[]{:S(2)}) collective-permute-start(bf16[17,16,128]{2,1,0:T(8,128)(2,1)S(1)} %get-tuple-element.43), channel_id=1, source_target_pairs={{0,4},{1,5},{2,6},{3,7},{4,0},{5,1},{6,2},{7,3},{8,12},{9,13},{10,... | collective-permute-start | bytes 208904 | tf_op jit(solution)/shard_map/ppermute | solution.py:236

commit v2 on v1

v2 whole, which is shorter than its diff:
```python
import functools
import math

import jax
import jax.numpy as jnp
from jax import lax
from jax.experimental import pallas as pl
from jax.experimental.pallas import tpu as pltpu
from jax.sharding import PartitionSpec as P

WINDOW = 8
DRAFT = 2
BLOCK_ROWS = 16
FLIPS = ((0,), (1,), (2, 3), (4,), (5,), (6,), (7,))
STAGE_FLOPS = 10_000_000_000
LOCAL_FLOPS = 20_000_000_000
VMEM_BYTES = 16 * 1024 * 1024


def nt_dot(left, right):
    return lax.dot_general(left, right, (((1,), (1,)), ((), ())), preferred_element_type=jnp.float32)


def local_kernel(len_ref, q_ref, kv_ref, out_ref, lse_ref, scores):
    rows, vectors, head_dim = q_ref.shape
    slots = kv_ref.shape[2]
    cached = slots - 16
    scaling = head_dim ** (-0.5)
    place = lax.broadcasted_iota(jnp.int32, (vectors, slots), 1)
    token = lax.broadcasted_iota(jnp.int32, (vectors, slots), 0) // (vectors // DRAFT)
    fresh = (place >= cached) & (place - cached <= token)
    for row in range(rows):
        live = (place < jnp.minimum(len_ref[row], cached)) | fresh
        scores[row] = jnp.where(live, nt_dot(q_ref[row], kv_ref[row, 0]) * scaling, -jnp.inf)
    maxima = scores[...].max(-1, keepdims=True)
    weights = jnp.exp(scores[...] - maxima)
    totals = weights.sum(-1, keepdims=True)
    lse_ref[...] = jnp.broadcast_to(maxima + jnp.log(totals), lse_ref.shape)
    inverse = 1.0 / totals
    rounded = weights.astype(jnp.bfloat16)
    for row in range(rows):
        summed = jnp.dot(rounded[row], kv_ref[row, 1], preferred_element_type=jnp.float32)
        out_ref[row] = summed * inverse[row]


def local_attention(queries, own_kv, new_kv, own_len):
    rows, vectors, head_dim = queries.shape
    cache = jnp.concatenate([own_kv, new_kv], axis=1)
    cache = jnp.pad(cache, ((0, 0), (0, 16 - DRAFT), (0, 0), (0, 0)))
    cache = cache.transpose(0, 2, 1, 3)
    shape = jax.ShapeDtypeStruct((rows, vectors, head_dim), jnp.float32)
    vmem = pl.BlockSpec(memory_space=pltpu.VMEM)
    return pl.pallas_call(
        local_kernel,
        out_shape=(shape, shape),
        in_specs=[pl.BlockSpec(memory_space=pltpu.SMEM), vmem, vmem],
        out_specs=(vmem, vmem),
        scratch_shapes=[pltpu.VMEM((rows, vectors, cache.shape[2]), jnp.float32)],
        compiler_params=pltpu.CompilerParams(vmem_limit_bytes=VMEM_BYTES),
        cost_estimate=pl.CostEstimate(flops=LOCAL_FLOPS, bytes_accessed=2_500_000, transcendentals=70_000),
        name="local_attention",
    )(own_len, queries, cache)


def attend_block(q, kv_refs, scores):
    width, head_dim = q.shape
    scaling = head_dim ** (-0.5)
    maxima = None
    for part, kv in enumerate(kv_refs):
        product = nt_dot(q, kv[0])
        scores[part] = product
        top = product.max(-1, keepdims=True)
        maxima = top if maxima is None else jnp.maximum(maxima, top)
    base2 = scaling * math.log2(math.e)
    shift = maxima * base2
    totals = jnp.zeros((width, 1), jnp.float32)
    summed = jnp.zeros((width, head_dim), jnp.float32)
    for part, kv in enumerate(kv_refs):
        weights = jnp.exp2(scores[part] * base2 - shift)
        totals = totals + weights.sum(-1, keepdims=True)
        summed = summed + jnp.dot(weights.astype(jnp.bfloat16), kv[1], preferred_element_type=jnp.float32)
    level = jnp.broadcast_to(maxima * scaling + jnp.log(totals), (width, head_dim))
    return summed / totals, level


def pack_kernel(live_ref, q_ref, packed, index):
    cells, tiles, vectors, head_dim = q_ref.shape
    rows = tiles - 1
    packed[...] = jnp.zeros_like(packed)
    count = jnp.int32(0)
    for slot in range(cells * rows):
        packed[count] = q_ref[slot // rows, slot % rows]
        index[count] = slot
        count = count + live_ref[slot]
    index[cells * rows + 1] = count


def pack_queries(live, arrived):
    cells, tiles, vectors, head_dim = arrived.shape
    slots = cells * (tiles - 1)
    vmem, smem = pl.BlockSpec(memory_space=pltpu.VMEM), pl.BlockSpec(memory_space=pltpu.SMEM)
    return pl.pallas_call(
        pack_kernel,
        out_shape=(
            jax.ShapeDtypeStruct((slots + BLOCK_ROWS, vectors, head_dim), jnp.bfloat16),
            jax.ShapeDtypeStruct((slots + 2,), jnp.int32),
        ),
        in_specs=[smem, vmem],
        out_specs=(vmem, smem),
        compiler_params=pltpu.CompilerParams(vmem_limit_bytes=VMEM_BYTES),
        name="pack_queries",
    )(live, arrived)


def merged(first, second):
    top = jnp.maximum(first[1], second[1])
    first_scale, second_scale = jnp.exp(first[1] - top), jnp.exp(second[1] - top)
    totals = first_scale + second_scale
    return (first[0] * first_scale + second[0] * second_scale) / totals, top + jnp.log(totals)


def stage_kernel(parts, halves, index, packed, *rest):
    state, kv_refs, outs, scores = rest[: 2 * parts], rest[2 * parts : -3], rest[-3:-1], rest[-1]
    kv_refs = [kv if half is None else kv.at[half] for kv, half in zip(kv_refs, halves)]
    width, head_dim = outs[0].shape[1:]
    count = index[index.shape[0] - 1]

    def block(step, carry):
        q = packed[pl.ds(step * BLOCK_ROWS, BLOCK_ROWS)].reshape(width, head_dim)
        total = attend_block(q, kv_refs, scores)
        if parts:
            total = merged(total, (state[0][step], state[1][step]))
        outs[0][step], outs[1][step] = total
        return carry

    lax.fori_loop(0, (count + BLOCK_ROWS - 1) // BLOCK_ROWS, block, 0)


def attend_stage(index, packed, state, blocks, halves=(None, None)):
    slots, vectors, head_dim = packed.shape[0] - BLOCK_ROWS, *packed.shape[1:]
    chunk = blocks[0].shape[-2]
    width = BLOCK_ROWS * vectors
    vmem, smem = pl.BlockSpec(memory_space=pltpu.VMEM), pl.BlockSpec(memory_space=pltpu.SMEM)
    shape = jax.ShapeDtypeStruct((slots // BLOCK_ROWS, width, head_dim), jnp.float32)
    return pl.pallas_call(
        functools.partial(stage_kernel, len(state) // 2, halves),
        out_shape=(shape, shape),
        in_specs=[smem] + [vmem] * (1 + len(state) + len(blocks)),
        out_specs=(vmem, vmem),
        scratch_shapes=[pltpu.VMEM((len(blocks), width, chunk), jnp.float32)],
        compiler_params=pltpu.CompilerParams(vmem_limit_bytes=VMEM_BYTES),
        cost_estimate=pl.CostEstimate(flops=STAGE_FLOPS, bytes_accessed=2_000_000, transcendentals=0),
        name="attend_stage",
    )(index, packed, *state, *blocks)


def late_kernel(index, packed, attended_ref, level_ref, *rest):
    *kv_refs, out_ref, scores, stats = rest
    cells, tiles, vectors, head_dim = out_ref.shape
    rows = tiles - 1
    width = BLOCK_ROWS * vectors
    out_ref[...] = jnp.zeros_like(out_ref)
    stats[...] = jnp.zeros_like(stats)
    count = index[cells * rows + 1]

    lane = lax.broadcasted_iota(jnp.int32, (vectors, head_dim), 1)
    vector = lax.broadcasted_iota(jnp.int32, (vectors, head_dim), 0)
    on_lane = (lane % vectors == vector) & (lane < 3 * vectors)
    piece = lane // vectors

    def block(step, carry):
        first = step * BLOCK_ROWS
        q = packed[pl.ds(first, BLOCK_ROWS)].reshape(width, head_dim)
        late = attend_block(q, kv_refs, scores)
        attended, level = merged(late, (attended_ref[step], level_ref[step]))
        attended = attended.astype(jnp.bfloat16)
        high = level.astype(jnp.bfloat16).astype(jnp.float32)
        middle = (level - high).astype(jnp.bfloat16).astype(jnp.float32)
        low = level - high - middle
        for row in range(BLOCK_ROWS):
            span = slice(row * vectors, (row + 1) * vectors)
            pieces = jnp.where(piece == 0, high[span], jnp.where(piece == 1, middle[span], low[span]))
            line = jnp.where(on_lane, pieces, 0.0).sum(0, keepdims=True)

            @pl.when(first + row < count)
            def _(row=row, span=span, line=line):
                slot = index[first + row]
                out_ref[slot // rows, slot % rows] = attended[span]
                stats[pl.ds(slot, 1), :] = line

        return carry

    lax.fori_loop(0, (count + BLOCK_ROWS - 1) // BLOCK_ROWS, block, 0)
    for cell in range(cells):
        out_ref[cell, rows] = stats[cell * rows : (cell + 1) * rows, :].astype(jnp.bfloat16)


def attend_late(shape, index, packed, state, blocks):
    cells, tiles, vectors, head_dim = shape
    slots = cells * (tiles - 1)
    chunk = blocks[0].shape[-2]
    width = BLOCK_ROWS * vectors
    vmem, smem = pl.BlockSpec(memory_space=pltpu.VMEM), pl.BlockSpec(memory_space=pltpu.SMEM)
    return pl.pallas_call(
        late_kernel,
        out_shape=jax.ShapeDtypeStruct(shape, jnp.bfloat16),
        in_specs=[smem] + [vmem] * (3 + len(blocks)),
        out_specs=vmem,
        scratch_shapes=[
            pltpu.VMEM((len(blocks), width, chunk), jnp.float32),
            pltpu.VMEM((slots, head_dim), jnp.float32),
        ],
        compiler_params=pltpu.CompilerParams(vmem_limit_bytes=VMEM_BYTES),
        cost_estimate=pl.CostEstimate(flops=STAGE_FLOPS, bytes_accessed=4_000_000, transcendentals=0),
        name="attend_late",
    )(index, packed, *state, *blocks)


def merge_kernel(*refs):
    *part_refs, local_ref, local_lse_ref, out_ref = refs
    rows, vectors, head_dim = local_ref.shape
    lane = lax.broadcasted_iota(jnp.int32, (vectors, head_dim), 1)
    vector = lax.broadcasted_iota(jnp.int32, (vectors, head_dim), 0)
    on_lane = (lane % vectors == vector) & (lane < 3 * vectors)
    pairs = [part_refs[k : k + 2] for k in range(0, len(part_refs), 2)]
    levels = [one[rows].astype(jnp.float32) + other[rows].astype(jnp.float32) for one, other in pairs]
    for row in range(rows):
        terms = [(local_ref[row], local_lse_ref[row])]
        for (one, other), level in zip(pairs, levels):
            line = jnp.broadcast_to(level[row : row + 1], (vectors, head_dim))
            lse = jnp.where(on_lane, line, 0.0).sum(-1, keepdims=True)
            attended = one[row].astype(jnp.float32) + other[row].astype(jnp.float32)
            terms.append((attended, jnp.broadcast_to(lse, (vectors, head_dim))))
        maxima = functools.reduce(jnp.maximum, [lse for _, lse in terms])
        scales = [jnp.exp(lse - maxima) for _, lse in terms]
        summed = sum(scale * term for scale, (term, _) in zip(scales, terms))
        out_ref[row] = (summed / sum(scales)).astype(jnp.bfloat16)


def merge_parts(parts, local, local_lse):
    vmem = pl.BlockSpec(memory_space=pltpu.VMEM)
    return pl.pallas_call(
        merge_kernel,
        out_shape=jax.ShapeDtypeStruct(local.shape, jnp.bfloat16),
        in_specs=[vmem] * (len(parts) + 2),
        out_specs=vmem,
        compiler_params=pltpu.CompilerParams(vmem_limit_bytes=VMEM_BYTES),
        name="merge_parts",
    )(*parts, local, local_lse)


def split_kernel(lane_ref, prefix_ref, *rest):
    *out_refs, by_head = rest
    sides = prefix_ref.shape[1]
    for side in range(sides):
        by_head[side] = jnp.swapaxes(prefix_ref[:, side], 0, 1)
    for out_ref, flips in zip(out_refs, FLIPS):
        for half, flip in enumerate(flips):
            for side in range(sides):
                target = out_ref if len(flips) == 1 else out_ref.at[half]
                target[side] = by_head[side, lane_ref[0] ^ flip]


def split_prefix(lane, prefix):
    positions, sides, heads, head_dim = prefix.shape
    shape = (sides, positions, head_dim)
    vmem = pl.BlockSpec(memory_space=pltpu.VMEM)
    return pl.pallas_call(
        split_kernel,
        out_shape=[
            jax.ShapeDtypeStruct(shape if len(flips) == 1 else (len(flips), *shape), prefix.dtype)
            for flips in FLIPS
        ],
        in_specs=[pl.BlockSpec(memory_space=pltpu.SMEM), vmem],
        out_specs=[vmem] * len(FLIPS),
        scratch_shapes=[pltpu.VMEM((sides, heads, positions, head_dim), prefix.dtype)],
        compiler_params=pltpu.CompilerParams(vmem_limit_bytes=VMEM_BYTES),
        cost_estimate=pl.CostEstimate(flops=0, bytes_accessed=4 * 1024 * 1024, transcendentals=0),
        name="split_prefix",
    )(lane.reshape(1), prefix)


def moved(x, by, flip=0):
    groups, lanes = lax.axis_size("group"), lax.axis_size("tensor")
    pairs = [
        (g * lanes + t, (g + by) % groups * lanes + (t ^ flip)) for g in range(groups) for t in range(lanes)
    ]
    return lax.ppermute(x, ("group", "tensor"), pairs)


def windowed(x):
    groups = lax.axis_size("group")
    windows = [list(range(first, first + WINDOW)) for first in range(0, groups, WINDOW)]
    return lax.all_to_all(x, "group", 0, 0, axis_index_groups=windows, tiled=True)


def on_device(queries, new_kv, own_kv, prefix_kv, owner, parent, own_len):
    rows, draft, width = queries.shape
    heads, head_dim = prefix_kv.shape[3:]
    per_kv = width // head_dim
    vectors = draft * per_kv
    me = lax.axis_index("group")
    place = me % WINDOW
    cells = jnp.arange(WINDOW)

    q = queries.reshape(rows, vectors, head_dim)
    distance = (me - owner[parent]) % lax.axis_size("group")
    tag = jnp.broadcast_to(distance.astype(jnp.bfloat16)[None, :, None], (1, rows, head_dim))
    sent = jnp.concatenate([q, tag.reshape(1, vectors, head_dim)])
    own, beside, near, *far = split_prefix(lax.axis_index("tensor"), prefix_kv[0])
    far = [moved(block, 0, 4 + step) for step, block in enumerate(far)]
    beside, sent = lax.optimization_barrier((moved(beside, 0, 1), sent))
    near, after = moved(near, 0, 2), moved(sent, -WINDOW)

    mine = (cells < place)[:, None, None, None]
    cell = jnp.where(mine, sent, after)
    arrived = windowed(cell)
    tags = arrived[:, rows, :, 0].astype(jnp.int32)
    live = (tags > 0) & (tags == ((cells - place) % WINDOW)[:, None])
    own_kv, new_kv, cell = lax.optimization_barrier((own_kv, new_kv, cell))
    late_q, near = lax.optimization_barrier((q, near))
    local, local_lse = local_attention(late_q, own_kv, new_kv, own_len)
    arrived, local, local_lse = lax.optimization_barrier((arrived, local, local_lse))
    packed, index = pack_queries(live.reshape(-1).astype(jnp.int32), arrived)
    near_beside = moved(near, 0, 1)
    state = attend_stage(index, packed, (), [own, beside, near, near_beside], (None, None, 0, 1))
    state = attend_stage(index, packed, state, far[:3], (None,) * 3)
    partial = attend_late(arrived.shape, index, packed, state, far[3:])

    returned = windowed(partial)
    here = jnp.where(mine, returned, 0).sum(0)
    after = moved(jnp.where(mine, 0, returned).sum(0), WINDOW)
    return merge_parts([here, after], local, local_lse).reshape(rows, draft, width)


def solution(mesh):
    placed = (
        P("group", None, "tensor"),
        P("group", None, None, "tensor"),
        P("group", None, None, "tensor"),
        P("group", "tensor", None, None, None),
        P(),
        P("group"),
        P("group"),
    )
    return jax.shard_map(
        on_device, mesh=mesh, in_specs=placed, out_specs=P("group", None, "tensor"), check_vma=False
    )
```

time: 107 us -> 96.7 us (0.904)
  blocking collectives: 24.9 us -> 12.9 us
  starting transfers between devices: 37.9 us -> 43.1 us
  local copies, waits for them, and re-layouts: 8.32 us -> 6.34 us
  waiting for transfers between devices: 19.7 us -> 18.2 us
    all_to_all x1, blocking collectives: 24.9 us -> 12.9 us  [windowed(): lax.all_to_all(x, 'group', 0, 0, axis_index_groups=windows, tiled=True)]
    ppermute x8 -> x9, starting transfers between devices: 33.8 us -> 39.1 us  [moved(): return lax.ppermute(x, ('group', 'tensor'), pairs)]
    ppermute x8 -> x9, waiting for transfers between devices: 19.7 us -> 14.5 us  [moved(): return lax.ppermute(x, ('group', 'tensor'), pairs)]
    all_to_all x1, waiting for transfers between devices: 0.01 us -> 3.67 us  [windowed(): lax.all_to_all(x, 'group', 0, 0, axis_index_groups=windows, tiled=True)]
    pallas_call x1, Pallas kernels: 4.53 us -> 1.24 us  [local_attention(): pl.pallas_call(local_kernel, out_shape=(shape, shape), in_specs=[pl.Block...]
    unnamed x18 -> x14, local copies, waits for them, and re-layouts: 5.81 us -> 2.57 us
    pallas_call x3 -> x5, Pallas kernels: 7.4 us -> 10.6 us  [the longest x2 5.63 us: attend_stage(): pl.pallas_call(functools.partial(stage_kernel, len(state) // 2, halves),...]
    optimization_barrier x0 -> x2, local copies, waits for them, and re-layouts: none -> 2.11 us  [on_device(): own_kv, new_kv, cell = lax.optimization_barrier((own_kv, new_kv, cell))]
  transfers between devices with their start and end apart: 9 -> 10, of which waited for: 3 -> 3; matrix products, arithmetic and copies ran while one was open for 6% -> 5% of each run, Pallas kernels for 6% -> 9%
where the time goes in v2:
time: 96.7 us; the launch traced here: 95.2 us
  starting transfers between devices  43.1 us (45%)
  waiting for transfers between devices  18.2 us (19%)
  blocking collectives  12.9 us (13%)
  Pallas kernels  12 us (12%)
  local copies, waits for them, and re-layouts  6.34 us (7%)
  other arithmetic  2.29 us (2%)
    ppermute x9, starting transfers between devices, moved(): return lax.ppermute(x, ('group', 'tensor'), pairs)  39.1 us
    ppermute x9, waiting for transfers between devices, moved(): return lax.ppermute(x, ('group', 'tensor'), pairs)  14.5 us
    all_to_all x1, blocking collectives, windowed(): lax.all_to_all(x, 'group', 0, 0, axis_index_groups=windows, tiled=True)  12.9 us
    pallas_call x2, Pallas kernels, attend_stage(): pl.pallas_call(functools.partial(stage_kernel, len(state) // 2, halves),...  5.63 us
    all_to_all x1, starting transfers between devices, windowed(): lax.all_to_all(x, 'group', 0, 0, axis_index_groups=windows, tiled=True)  4.02 us
    all_to_all x1, waiting for transfers between devices, windowed(): lax.all_to_all(x, 'group', 0, 0, axis_index_groups=windows, tiled=True)  3.67 us
    unnamed x14, local copies, waits for them, and re-layouts  2.57 us
    pallas_call x1, Pallas kernels, attend_late(): pl.pallas_call(late_kernel, out_shape=jax.ShapeDtypeStruct(shape, jnp.bfl...  2.51 us
  transfers between devices with their start and end apart: 10, of which 3 were waited for; matrix products, arithmetic and copies ran while one was open for 5% of the time, Pallas kernels for 9%

profile of v2, /device:TPU:1, one launch (start us, length us, event | category | flops | bytes accessed | tf_op | source)
XLA Modules:
  0.0 95.2 jit_solution(12669691130799573949)
XLA Ops:
  0.0 0.0 copy-start
  0.0 0.0 copy-start.1
  0.0 1.6 %copy-done.1 = bf16[1,512,2,8,128]{4,3,2,1,0:T(8,128)(2,1)S(1)} copy-done((bf16[1,512,2,8,128]{4,3,2,1,0:T(8,128)(2,1)S(1)}, bf16[1,512,2,8,128]{4,3,2,1,0:T(8,128)(2,1)}, u32[]{:S(2)}) %copy-start.1) | copy-done | bytes 2097176
  1.6 0.0 copy-start.5
  1.6 1.0 %split_prefix.1 = (bf16[2,512,128]{2,1,0:T(8,128)(2,1)S(1)}, bf16[2,512,128]{2,1,0:T(8,128)(2,1)S(1)}, bf16[2,2,512,128]{3,2,1,0:T(8,128)(2,1)S(1)}, bf16[2,512,...) custom-call(s32[1]{0:T(128)} %bitcast.lane_ref, ...), custom_call_target="tpu_custom_call" | custom-call | bytes 4194304 | tf_op jit(solution)/shard_map/split_prefix/pallas_call | solution.py:268
  2.6 8.8 %collective-permute-start = (bf16[2,512,128]{2,1,0:T(8,128)(2,1)S(1)}, bf16[2,512,128]{2,1,0:T(8,128)(2,1)S(1)}, u32[]{:S(2)}, u32[]{:S(2)}) collective-permute-start(bf16[2,512,128]{2,1,0:T(8,128)(2,1)S(1)} %get-tuple-element.29), channel_id=1, source_target_pairs={{0,1},{1,0},{2,3},{3,2},{4,5},{5,4},{6,7},{7,6},{8,9},{9,8},{10,11... | collective-permute-start | bytes 786440 | tf_op jit(solution)/shard_map/ppermute | solution.py:288
  11.4 1.9 %collective-permute-start.2 = (bf16[2,2,512,128]{3,2,1,0:T(8,128)(2,1)S(1)}, bf16[2,2,512,128]{3,2,1,0:T(8,128)(2,1)S(1)}, u32[]{:S(2)}, u32[]{:S(2)}) collective-permute-start(bf16[2,2,512,128]{3,2,1,0:T(8,128)(2,1)S(1)} %get-tuple-element.31), channel_id=1, source_target_pairs={{0,2},{1,3},{2,0},{3,1},{4,6},{5,7},{6,4},{7,5},{8,10},{9,11},{10,... | collective-permute-start | bytes 1572872 | tf_op jit(solution)/shard_map/ppermute | solution.py:288
  13.3 2.5 %collective-permute-start.4 = (bf16[2,512,128]{2,1,0:T(8,128)(2,1)S(1)}, bf16[2,512,128]{2,1,0:T(8,128)(2,1)S(1)}, u32[]{:S(2)}, u32[]{:S(2)}) collective-permute-start(bf16[2,512,128]{2,1,0:T(8,128)(2,1)S(1)} %get-tuple-element.45), channel_id=1, source_target_pairs={{0,4},{1,5},{2,6},{3,7},{4,0},{5,1},{6,2},{7,3},{8,12},{9,13},{10,... | collective-permute-start | bytes 786440 | tf_op jit(solution)/shard_map/ppermute | solution.py:288
  15.8 3.8 %collective-permute-start.5 = (bf16[2,512,128]{2,1,0:T(8,128)(2,1)S(1)}, bf16[2,512,128]{2,1,0:T(8,128)(2,1)}, u32[]{:S(2)}, u32[]{:S(2)}) collective-permute-start(bf16[2,512,128]{2,1,0:T(8,128)(2,1)S(1)} %get-tuple-element.46), channel_id=1, source_target_pairs={{0,5},{1,4},{2,7},{3,6},{4,1},{5,0},{6,3},{7,2},{8,13},{9,12},{10,... | collective-permute-start | bytes 786440 | tf_op jit(solution)/shard_map/ppermute | solution.py:288
  19.7 3.1 %collective-permute-start.6 = (bf16[2,512,128]{2,1,0:T(8,128)(2,1)S(1)}, bf16[2,512,128]{2,1,0:T(8,128)(2,1)}, u32[]{:S(2)}, u32[]{:S(2)}) collective-permute-start(bf16[2,512,128]{2,1,0:T(8,128)(2,1)S(1)} %get-tuple-element.47), channel_id=1, source_target_pairs={{0,6},{1,7},{2,4},{3,5},{4,2},{5,3},{6,0},{7,1},{8,14},{9,15},{10,... | collective-permute-start | bytes 786440 | tf_op jit(solution)/shard_map/ppermute | solution.py:288
  22.8 0.7 compare_select_fusion
  23.5 0.0 copy-done
  23.5 0.7 gather_fusion
  24.2 0.0 copy-done.5
  24.2 0.1 broadcast_in_dim.47
  24.3 0.0 collective-permute-done.rest_1_
  24.3 0.0 copy-start.2
  24.3 11.3 %collective-permute-start.1 = (bf16[17,16,128]{2,1,0:T(8,128)(2,1)S(1)}, bf16[17,16,128]{2,1,0:T(8,128)(2,1)S(1)}, u32[]{:S(2)}, u32[]{:S(2)}) collective-permute-start(bf16[17,16,128]{2,1,0:T(8,128)(2,1)S(1)} %pad_maximum_fusion), channel_id=1, source_target_pairs={{0,448},{1,449},{2,450},{3,451},{4,452},{5,453},{6,454},{7,455},{8... | collective-permute-start | bytes 208904 | tf_op jit(solution)/shard_map/ppermute | solution.py:288
  35.7 0.1 eq.17
  35.8 0.1 eq.18
  35.8 2.9 %collective-permute-done.1 = bf16[17,16,128]{2,1,0:T(8,128)(2,1)S(1)} collective-permute-done((bf16[17,16,128]{2,1,0:T(8,128)(2,1)S(1)}, bf16[17,16,128]{2,1,0:T(8,128)(2,1)S(1)}, u32[]{:S(2)}, u32[]{:S(2)}) %collective-permute-start.1) | collective-permute-done | bytes 69664 | tf_op jit(solution)/shard_map/ppermute | solution.py:288
  38.8 3.7 %collective-permute-start.7 = (bf16[2,512,128]{2,1,0:T(8,128)(2,1)S(1)}, bf16[2,512,128]{2,1,0:T(8,128)(2,1)}, u32[]{:S(2)}, u32[]{:S(2)}) collective-permute-start(bf16[2,512,128]{2,1,0:T(8,128)(2,1)S(1)} %get-tuple-element.50), channel_id=1, source_target_pairs={{0,7},{1,6},{2,5},{3,4},{4,3},{5,2},{6,1},{7,0},{8,15},{9,14},{10,... | collective-permute-start | bytes 786440 | tf_op jit(solution)/shard_map/ppermute | solution.py:288
  42.5 0.9 broadcast_select_fusion
  43.4 4.0 %all-to-all-start = ((bf16[8,17,16,128]{3,2,1,0:T(8,128)(2,1)}), bf16[8,17,16,128]{3,2,1,0:T(8,128)(2,1)S(1)}, u32[]{:S(2)}, u32[]{:S(2)}) async-start(bf16[8,17,16,128]{3,2,1,0:T(8,128)(2,1)} %broadcast_select_fusion), calls=%async_computation | async-start | bytes 1114112 | tf_op jit(solution)/shard_map/all_to_all | solution.py:294
  47.4 0.0 copy-start.6
  47.4 2.1 %copy.10 = bf16[16,256,2,128]{3,1,2,0:T(8,128)(2,1)S(1)} copy(bf16[16,256,2,128]{3,2,1,0:T(2,128)(2,1)} %param.9) | data formatting | bytes 4194304 | tf_op jit(solution)/shard_map/optimization_barrier | solution.py:320
  49.5 0.0 copy-done.2
  49.5 0.0 copy-done.6
  49.6 0.0 copy-start.4
  49.6 0.2 fusion.3.kv_ref
  49.8 0.0 collective-permute-done.2.rest_2_
  49.8 1.9 %collective-permute-start.3 = (bf16[2,2,512,128]{3,2,1,0:T(8,128)(2,1)S(1)}, bf16[2,2,512,128]{3,2,1,0:T(8,128)(2,1)S(1)}, u32[]{:S(2)}, u32[]{:S(2)}) collective-permute-start(bf16[2,2,512,128]{3,2,1,0:T(8,128)(2,1)S(1)} %collective-permute-done.2.rest_2_), channel_id=1, source_target_pairs={{0,1},{1,0},{2,3},{3,2},{4,5},{5,4},{6,7},{7,6},{8,9},{9,8},{10,11... | collective-permute-start | bytes 1572872 | tf_op jit(solution)/shard_map/ppermute | solution.py:288
  51.8 0.0 copy-done.4
  51.8 1.2 %local_attention.1 = (f32[16,16,128]{2,1,0:T(8,128)S(1)}, f32[16,16,128]{2,1,0:T(8,128)S(1)}) custom-call(s32[16]{0:T(128)S(1)} %copy-done.4, bf16[16,16,128]{2,1,0:T(8,128)(2,1)S(1)} %reshape.51.q_ref, bf16[16,2,272,128]{3,2,1,0:T(8,128)(2,1)S(1)} %fusion.3.kv_ref), custom_call_target="tpu_custom_call" | custom-call | flops 20000000000 | bytes 2500000 | tf_op jit(solution)/shard_map/local_attention/pallas_call | solution.py:53
  53.0 3.7 %all-to-all-done.q_ref = bf16[8,17,16,128]{3,2,1,0:T(8,128)(2,1)S(1)} async-done(((bf16[8,17,16,128]{3,2,1,0:T(8,128)(2,1)}), bf16[8,17,16,128]{3,2,1,0:T(8,128)(2,1)S(1)}, u32[]{:S(2)}, u32[]{:S(2)}) %all-to-all-start) | async-done | bytes 557088 | tf_op jit(solution)/shard_map/all_to_all | solution.py:294
  56.7 0.2 convert_reduce_fusion
  56.9 0.1 reshape.53
  57.0 1.5 %pack_queries.1 = (bf16[144,16,128]{2,1,0:T(8,128)(2,1)S(1)}, s32[130]{0:T(256)S(1)}) custom-call(s32[128]{0:T(128)S(1)} %and_convert_fusion.live_ref, bf16[8,17,16,128]{3,2,1,0:T(8,128)(2,1)S(1)} %all-to-all-done.q_ref), custom_call_target="tpu_custom_call" | custom-call | tf_op jit(solution)/shard_map/pack_queries/pallas_call | solution.py:102
  58.5 0.0 collective-permute-done.3.rest_3_
  58.5 0.0 copy-start.3
  58.5 0.9 copy-done.3
  59.5 2.8 %attend_stage.2 = (f32[8,256,128]{2,1,0:T(8,128)S(1)}, f32[8,256,128]{2,1,0:T(8,128)S(1)}) custom-call(s32[130]{0:T(256)S(1)} %get-tuple-element.38.index, bf16[144,16,128]{2,1,0:T(8,128)(2,1)S(1)} %get-tuple-element.39.packed, bf16[2,512,128]{2,1,0:T(8,128)(2,1)S(1)} %get-tuple-element.40.rest_0_, bf16[2,512,128]{2,1,0:T(8,128)(2,1)S(1)} %copy-done.3, ...), custom_call_target="tpu_custom_call" | custom-call | flops 10000000000 | bytes 2000000 | tf_op jit(solution)/shard_map/attend_stage/pallas_call | solution.py:145
  62.3 0.0 collective-permute-done.4.rest_2_
  62.3 0.0 collective-permute-done.5.rest_3_
  62.3 0.0 collective-permute-done.6.rest_4_
  62.3 2.8 %attend_stage.3 = (f32[8,256,128]{2,1,0:T(8,128)S(1)}, f32[8,256,128]{2,1,0:T(8,128)S(1)}) custom-call(s32[130]{0:T(256)S(1)} %get-tuple-element.38.index, bf16[144,16,128]{2,1,0:T(8,128)(2,1)S(1)} %get-tuple-element.39.packed, f32[8,256,128]{2,1,0:T(8,128)S(1)} %get-tuple-element.43.rest_0_, f32[8,256,128]{2,1,0:T(8,128)S(1)} %get-tuple-element.44.rest_1_, ...), custom_call_target="tpu_custom_call" | custom-call | flops 10000000000 | bytes 2000000 | tf_op jit(solution)/shard_map/attend_stage/pallas_call | solution.py:145
  65.1 0.0 collective-permute-done.7.rest_0_
  65.2 2.5 %attend_late.1 = bf16[8,17,16,128]{3,2,1,0:T(8,128)(2,1)S(1)} custom-call(s32[130]{0:T(256)S(1)} %get-tuple-element.38.index, bf16[144,16,128]{2,1,0:T(8,128)(2,1)S(1)} %get-tuple-element.39.packed, f32[8,256,128]{2,1,0:T(8,128)S(1)} %get-tuple-element.48.attended_ref, f32[8,256,128]{2,1,0:T(8,128)S(1)} %get-tuple-element.49.level_ref, ...), custom_call_target="tpu_custom_call" | custom-call | flops 10000000000 | bytes 4000000 | tf_op jit(solution)/shard_map/attend_late/pallas_call | solution.py:204
  67.7 12.9 %all_to_all.10 = bf16[8,17,16,128]{3,2,1,0:T(8,128)(2,1)S(1)} all-to-all(bf16[8,17,16,128]{3,2,1,0:T(8,128)(2,1)S(1)} %attend_late.1), channel_id=1, replica_groups={{0,8,16,24,32,40,48,56},{64,72,80,88,96,104,112,120},{128,136,144,152,1..., dimensions={0} | all-to-all | bytes 1114112 | tf_op jit(solution)/shard_map/all_to_all | solution.py:294
  80.6 0.3 select_reduce_fusion
  80.9 1.9 %collective-permute-start.8 = (bf16[17,16,128]{2,1,0:T(8,128)(2,1)S(1)}, bf16[17,16,128]{2,1,0:T(8,128)(2,1)S(1)}, u32[]{:S(2)}, u32[]{:S(2)}) collective-permute-start(bf16[17,16,128]{2,1,0:T(8,128)(2,1)S(1)} %get-tuple-element.53), channel_id=1, source_target_pairs={{0,64},{1,65},{2,66},{3,67},{4,68},{5,69},{6,70},{7,71},{8,72},{9,... | collective-permute-start | bytes 208904 | tf_op jit(solution)/shard_map/ppermute | solution.py:288
  82.8 11.6 %collective-permute-done.8.refs_1_ = bf16[17,16,128]{2,1,0:T(8,128)(2,1)S(1)} collective-permute-done((bf16[17,16,128]{2,1,0:T(8,128)(2,1)S(1)}, bf16[17,16,128]{2,1,0:T(8,128)(2,1)S(1)}, u32[]{:S(2)}, u32[]{:S(2)}) %collective-permute-start.8) | collective-permute-done | bytes 69664 | tf_op jit(solution)/shard_map/ppermute | solution.py:288
  94.4 0.1 merge_parts.1
  94.5 0.7 reshape.52
  (8 shorter events, 0.1 us)
Async XLA Ops:
  0.0 23.5 %copy-start = (s32[64]{0:T(128)S(1)}, s32[64]{0:T(128)}, u32[]{:S(2)}) copy-start(s32[64]{0:T(128)} %param.11) | copy-start | bytes 772
  0.0 1.6 %copy-start.1 = (bf16[1,512,2,8,128]{4,3,2,1,0:T(8,128)(2,1)S(1)}, bf16[1,512,2,8,128]{4,3,2,1,0:T(8,128)(2,1)}, u32[]{:S(2)}) copy-start(bf16[1,512,2,8,128]{4,3,2,1,0:T(8,128)(2,1)} %param.10) | copy-start | bytes 6291460
  1.6 22.5 %copy-start.5 = (bf16[16,2,1024]{2,1,0:T(2,128)(2,1)S(1)}, bf16[16,2,1024]{2,1,0:T(2,128)(2,1)}, u32[]{:S(2)}) copy-start(bf16[16,2,1024]{2,1,0:T(2,128)(2,1)} %param.7) | copy-start | bytes 196612
  2.6 21.7 %collective-permute-start = (bf16[2,512,128]{2,1,0:T(8,128)(2,1)S(1)}, bf16[2,512,128]{2,1,0:T(8,128)(2,1)S(1)}, u32[]{:S(2)}, u32[]{:S(2)}) collective-permute-start(bf16[2,512,128]{2,1,0:T(8,128)(2,1)S(1)} %get-tuple-element.29), channel_id=1, source_target_pairs={{0,1},{1,0},{2,3},{3,2},{4,5},{5,4},{6,7},{7,6},{8,9},{9,8},{10,11... | collective-permute-start | bytes 786440 | tf_op jit(solution)/shard_map/ppermute | solution.py:288
  11.4 38.4 %collective-permute-start.2 = (bf16[2,2,512,128]{3,2,1,0:T(8,128)(2,1)S(1)}, bf16[2,2,512,128]{3,2,1,0:T(8,128)(2,1)S(1)}, u32[]{:S(2)}, u32[]{:S(2)}) collective-permute-start(bf16[2,2,512,128]{3,2,1,0:T(8,128)(2,1)S(1)} %get-tuple-element.31), channel_id=1, source_target_pairs={{0,2},{1,3},{2,0},{3,1},{4,6},{5,7},{6,4},{7,5},{8,10},{9,11},{10,... | collective-permute-start | bytes 1572872 | tf_op jit(solution)/shard_map/ppermute | solution.py:288
  13.3 49.0 %collective-permute-start.4 = (bf16[2,512,128]{2,1,0:T(8,128)(2,1)S(1)}, bf16[2,512,128]{2,1,0:T(8,128)(2,1)S(1)}, u32[]{:S(2)}, u32[]{:S(2)}) collective-permute-start(bf16[2,512,128]{2,1,0:T(8,128)(2,1)S(1)} %get-tuple-element.45), channel_id=1, source_target_pairs={{0,4},{1,5},{2,6},{3,7},{4,0},{5,1},{6,2},{7,3},{8,12},{9,13},{10,... | collective-permute-start | bytes 786440 | tf_op jit(solution)/shard_map/ppermute | solution.py:288
  15.8 46.5 %collective-permute-start.5 = (bf16[2,512,128]{2,1,0:T(8,128)(2,1)S(1)}, bf16[2,512,128]{2,1,0:T(8,128)(2,1)}, u32[]{:S(2)}, u32[]{:S(2)}) collective-permute-start(bf16[2,512,128]{2,1,0:T(8,128)(2,1)S(1)} %get-tuple-element.46), channel_id=1, source_target_pairs={{0,5},{1,4},{2,7},{3,6},{4,1},{5,0},{6,3},{7,2},{8,13},{9,12},{10,... | collective-permute-start | bytes 786440 | tf_op jit(solution)/shard_map/ppermute | solution.py:288
  19.7 42.6 %collective-permute-start.6 = (bf16[2,512,128]{2,1,0:T(8,128)(2,1)S(1)}, bf16[2,512,128]{2,1,0:T(8,128)(2,1)}, u32[]{:S(2)}, u32[]{:S(2)}) collective-permute-start(bf16[2,512,128]{2,1,0:T(8,128)(2,1)S(1)} %get-tuple-element.47), channel_id=1, source_target_pairs={{0,6},{1,7},{2,4},{3,5},{4,2},{5,3},{6,0},{7,1},{8,14},{9,15},{10,... | collective-permute-start | bytes 786440 | tf_op jit(solution)/shard_map/ppermute | solution.py:288
  24.3 25.2 %copy-start.2 = (bf16[2,512,128]{2,1,0:T(8,128)(2,1)}, bf16[2,512,128]{2,1,0:T(8,128)(2,1)S(1)}, u32[]{:S(2)}) copy-start(bf16[2,512,128]{2,1,0:T(8,128)(2,1)S(1)} %collective-permute-done.rest_1_) | copy-start | bytes 786436
  24.3 14.4 %collective-permute-start.1 = (bf16[17,16,128]{2,1,0:T(8,128)(2,1)S(1)}, bf16[17,16,128]{2,1,0:T(8,128)(2,1)S(1)}, u32[]{:S(2)}, u32[]{:S(2)}) collective-permute-start(bf16[17,16,128]{2,1,0:T(8,128)(2,1)S(1)} %pad_maximum_fusion), channel_id=1, source_target_pairs={{0,448},{1,449},{2,450},{3,451},{4,452},{5,453},{6,454},{7,455},{8... | collective-permute-start | bytes 208904 | tf_op jit(solution)/shard_map/ppermute | solution.py:288
  38.8 26.4 %collective-permute-start.7 = (bf16[2,512,128]{2,1,0:T(8,128)(2,1)S(1)}, bf16[2,512,128]{2,1,0:T(8,128)(2,1)}, u32[]{:S(2)}, u32[]{:S(2)}) collective-permute-start(bf16[2,512,128]{2,1,0:T(8,128)(2,1)S(1)} %get-tuple-element.50), channel_id=1, source_target_pairs={{0,7},{1,6},{2,5},{3,4},{4,3},{5,2},{6,1},{7,0},{8,15},{9,14},{10,... | collective-permute-start | bytes 786440 | tf_op jit(solution)/shard_map/ppermute | solution.py:288
  43.4 13.3 %all-to-all-start = ((bf16[8,17,16,128]{3,2,1,0:T(8,128)(2,1)}), bf16[8,17,16,128]{3,2,1,0:T(8,128)(2,1)S(1)}, u32[]{:S(2)}, u32[]{:S(2)}) async-start(bf16[8,17,16,128]{3,2,1,0:T(8,128)(2,1)} %broadcast_select_fusion), calls=%async_computation | async-start | bytes 1114112 | tf_op jit(solution)/shard_map/all_to_all | solution.py:294
  47.4 2.1 %copy-start.6 = (bf16[16,2,2,128]{3,2,1,0:T(2,128)(2,1)S(1)}, bf16[16,2,2,128]{3,2,1,0:T(2,128)(2,1)}, u32[]{:S(2)}) copy-start(bf16[16,2,2,128]{3,2,1,0:T(2,128)(2,1)} %param.8) | copy-start | bytes 49156
  49.6 2.2 %copy-start.4 = (s32[16]{0:T(128)S(1)}, s32[16]{0:T(128)}, u32[]{:S(2)}) copy-start(s32[16]{0:T(128)} %len_ref.1) | copy-start | bytes 196
  49.8 8.7 %collective-permute-start.3 = (bf16[2,2,512,128]{3,2,1,0:T(8,128)(2,1)S(1)}, bf16[2,2,512,128]{3,2,1,0:T(8,128)(2,1)S(1)}, u32[]{:S(2)}, u32[]{:S(2)}) collective-permute-start(bf16[2,2,512,128]{3,2,1,0:T(8,128)(2,1)S(1)} %collective-permute-done.2.rest_2_), channel_id=1, source_target_pairs={{0,1},{1,0},{2,3},{3,2},{4,5},{5,4},{6,7},{7,6},{8,9},{9,8},{10,11... | collective-permute-start | bytes 1572872 | tf_op jit(solution)/shard_map/ppermute | solution.py:288
  58.5 1.0 copy-start.3
  80.9 13.5 %collective-permute-start.8 = (bf16[17,16,128]{2,1,0:T(8,128)(2,1)S(1)}, bf16[17,16,128]{2,1,0:T(8,128)(2,1)S(1)}, u32[]{:S(2)}, u32[]{:S(2)}) collective-permute-start(bf16[17,16,128]{2,1,0:T(8,128)(2,1)S(1)} %get-tuple-element.53), channel_id=1, source_target_pairs={{0,64},{1,65},{2,66},{3,67},{4,68},{5,69},{6,70},{7,71},{8,72},{9,... | collective-permute-start | bytes 208904 | tf_op jit(solution)/shard_map/ppermute | solution.py:288

commit v3 on v2

--- a/solution.py
+++ b/solution.py
@@ -177,17 +177,12 @@
         high = level.astype(jnp.bfloat16).astype(jnp.float32)
         middle = (level - high).astype(jnp.bfloat16).astype(jnp.float32)
         low = level - high - middle
-        for row in range(BLOCK_ROWS):
+        for row in reversed(range(BLOCK_ROWS)):
             span = slice(row * vectors, (row + 1) * vectors)
             pieces = jnp.where(piece == 0, high[span], jnp.where(piece == 1, middle[span], low[span]))
-            line = jnp.where(on_lane, pieces, 0.0).sum(0, keepdims=True)
-
-            @pl.when(first + row < count)
-            def _(row=row, span=span, line=line):
-                slot = index[first + row]
-                out_ref[slot // rows, slot % rows] = attended[span]
-                stats[pl.ds(slot, 1), :] = line
-
+            slot = index[first + jnp.where(first + row < count, row, 0)]
+            out_ref[slot // rows, slot % rows] = attended[span]
+            stats[pl.ds(slot, 1), :] = jnp.where(on_lane, pieces, 0.0).sum(0, keepdims=True)
         return carry
 
     lax.fori_loop(0, (count + BLOCK_ROWS - 1) // BLOCK_ROWS, block, 0)
@@ -308,8 +303,8 @@
     tag = jnp.broadcast_to(distance.astype(jnp.bfloat16)[None, :, None], (1, rows, head_dim))
     sent = jnp.concatenate([q, tag.reshape(1, vectors, head_dim)])
     own, beside, near, *far = split_prefix(lax.axis_index("tensor"), prefix_kv[0])
-    far = [moved(block, 0, 4 + step) for step, block in enumerate(far)]
-    beside, sent = lax.optimization_barrier((moved(beside, 0, 1), sent))
+    beside, far[2], sent = lax.optimization_barrier((moved(beside, 0, 1), far[2], sent))
+    far[:3] = [moved(block, 0, 4 + step) for step, block in enumerate(far[:3])]
     near, after = moved(near, 0, 2), moved(sent, -WINDOW)
 
     mine = (cells < place)[:, None, None, None]
@@ -317,14 +312,15 @@
     arrived = windowed(cell)
     tags = arrived[:, rows, :, 0].astype(jnp.int32)
     live = (tags > 0) & (tags == ((cells - place) % WINDOW)[:, None])
-    own_kv, new_kv, cell = lax.optimization_barrier((own_kv, new_kv, cell))
-    late_q, near = lax.optimization_barrier((q, near))
+    own_kv, new_kv, far[3], cell = lax.optimization_barrier((own_kv, new_kv, far[3], cell))
+    far[3] = moved(far[3], 0, 7)
+    late_q, far[0] = lax.optimization_barrier((q, far[0]))
     local, local_lse = local_attention(late_q, own_kv, new_kv, own_len)
     arrived, local, local_lse = lax.optimization_barrier((arrived, local, local_lse))
     packed, index = pack_queries(live.reshape(-1).astype(jnp.int32), arrived)
     near_beside = moved(near, 0, 1)
-    state = attend_stage(index, packed, (), [own, beside, near, near_beside], (None, None, 0, 1))
-    state = attend_stage(index, packed, state, far[:3], (None,) * 3)
+    state = attend_stage(index, packed, (), [own, beside, far[0]], (None,) * 3)
+    state = attend_stage(index, packed, state, [near, near_beside, *far[1:3]], (0, 1, None, None))
     partial = attend_late(arrived.shape, index, packed, state, far[3:])
 
     returned = windowed(partial)

time: 96.7 us -> 94.1 us (0.973)
  the two profiles are of different devices: /device:TPU:1 before, /device:TPU:128 now
where the time goes in v3:
time: 94.1 us; the launch traced here: 93.4 us
  starting transfers between devices  38.7 us (41%)
  waiting for transfers between devices  20.5 us (22%)
  blocking collectives  15.5 us (16%)
  Pallas kernels  9.07 us (10%)
  local copies, waits for them, and re-layouts  7.17 us (8%)
  other arithmetic  2.29 us (2%)
    ppermute x9, starting transfers between devices, moved(): return lax.ppermute(x, ('group', 'tensor'), pairs)  34.4 us
    ppermute x9, waiting for transfers between devices, moved(): return lax.ppermute(x, ('group', 'tensor'), pairs)  18.7 us
    all_to_all x1, blocking collectives, windowed(): lax.all_to_all(x, 'group', 0, 0, axis_index_groups=windows, tiled=True)  15.5 us
    all_to_all x1, starting transfers between devices, windowed(): lax.all_to_all(x, 'group', 0, 0, axis_index_groups=windows, tiled=True)  4.3 us
    pallas_call x2, Pallas kernels, attend_stage(): pl.pallas_call(functools.partial(stage_kernel, len(state) // 2, halves),...  3.57 us
    unnamed x12, local copies, waits for them, and re-layouts  2.57 us
    optimization_barrier x2, local copies, waits for them, and re-layouts, on_device(): lax.optimization_barrier((own_kv, new_kv, far[3], cell))  2.11 us
  transfers between devices with their start and end apart: 10, of which 4 were waited for; matrix products, arithmetic and copies ran while one was open for 6% of the time, Pallas kernels for 7%

profile of v3, /device:TPU:128, one launch (start us, length us, event | category | flops | bytes accessed | tf_op | source)
XLA Modules:
  0.0 93.4 jit_solution(5946547486657861589)
XLA Ops:
  0.0 0.0 copy-start
  0.0 0.0 copy-start.1
  0.0 1.6 %copy-done.1 = bf16[1,512,2,8,128]{4,3,2,1,0:T(8,128)(2,1)S(1)} copy-done((bf16[1,512,2,8,128]{4,3,2,1,0:T(8,128)(2,1)S(1)}, bf16[1,512,2,8,128]{4,3,2,1,0:T(8,128)(2,1)}, u32[]{:S(2)}) %copy-start.1) | copy-done | bytes 2097176
  1.6 1.0 %split_prefix.1 = (bf16[2,512,128]{2,1,0:T(8,128)(2,1)S(1)}, bf16[2,512,128]{2,1,0:T(8,128)(2,1)S(1)}, bf16[2,2,512,128]{3,2,1,0:T(8,128)(2,1)S(1)}, bf16[2,512,...) custom-call(s32[1]{0:T(128)} %bitcast.lane_ref, ...), custom_call_target="tpu_custom_call" | custom-call | bytes 4194304 | tf_op jit(solution)/shard_map/split_prefix/pallas_call | solution.py:263
  2.6 1.9 %collective-permute-start = (bf16[2,512,128]{2,1,0:T(8,128)(2,1)S(1)}, bf16[2,512,128]{2,1,0:T(8,128)(2,1)S(1)}, u32[]{:S(2)}, u32[]{:S(2)}) collective-permute-start(bf16[2,512,128]{2,1,0:T(8,128)(2,1)S(1)} %get-tuple-element.31), channel_id=1, source_target_pairs={{0,1},{1,0},{2,3},{3,2},{4,5},{5,4},{6,7},{7,6},{8,9},{9,8},{10,11... | collective-permute-start | bytes 786440 | tf_op jit(solution)/shard_map/ppermute | solution.py:283
  4.5 6.0 %collective-permute-start.2 = (bf16[2,512,128]{2,1,0:T(8,128)(2,1)S(1)}, bf16[2,512,128]{2,1,0:T(8,128)(2,1)S(1)}, u32[]{:S(2)}, u32[]{:S(2)}) collective-permute-start(bf16[2,512,128]{2,1,0:T(8,128)(2,1)S(1)} %get-tuple-element.34), channel_id=1, source_target_pairs={{0,4},{1,5},{2,6},{3,7},{4,0},{5,1},{6,2},{7,3},{8,12},{9,13},{10,... | collective-permute-start | bytes 786440 | tf_op jit(solution)/shard_map/ppermute | solution.py:283
  10.5 1.9 %collective-permute-start.3 = (bf16[2,2,512,128]{3,2,1,0:T(8,128)(2,1)S(1)}, bf16[2,2,512,128]{3,2,1,0:T(8,128)(2,1)S(1)}, u32[]{:S(2)}, u32[]{:S(2)}) collective-permute-start(bf16[2,2,512,128]{3,2,1,0:T(8,128)(2,1)S(1)} %get-tuple-element.49), channel_id=1, source_target_pairs={{0,2},{1,3},{2,0},{3,1},{4,6},{5,7},{6,4},{7,5},{8,10},{9,11},{10,... | collective-permute-start | bytes 1572872 | tf_op jit(solution)/shard_map/ppermute | solution.py:283
  12.5 2.6 %collective-permute-start.5 = (bf16[2,512,128]{2,1,0:T(8,128)(2,1)S(1)}, bf16[2,512,128]{2,1,0:T(8,128)(2,1)S(1)}, u32[]{:S(2)}, u32[]{:S(2)}) collective-permute-start(bf16[2,512,128]{2,1,0:T(8,128)(2,1)S(1)} %get-tuple-element.50), channel_id=1, source_target_pairs={{0,5},{1,4},{2,7},{3,6},{4,1},{5,0},{6,3},{7,2},{8,13},{9,12},{10,... | collective-permute-start | bytes 786440 | tf_op jit(solution)/shard_map/ppermute | solution.py:283
  15.1 0.7 compare_select_fusion
  15.8 0.0 copy-done
  15.8 0.7 gather_fusion
  16.5 0.9 reshape.51.q_ref
  17.4 0.1 eq.17
  17.4 0.1 eq.18
  17.5 0.1 broadcast_in_dim.47
  17.6 0.0 collective-permute-done.rest_1_
  17.6 11.9 %collective-permute-start.1 = (bf16[17,16,128]{2,1,0:T(8,128)(2,1)S(1)}, bf16[17,16,128]{2,1,0:T(8,128)(2,1)S(1)}, u32[]{:S(2)}, u32[]{:S(2)}) collective-permute-start(bf16[17,16,128]{2,1,0:T(8,128)(2,1)S(1)} %pad_maximum_fusion), channel_id=1, source_target_pairs={{0,448},{1,449},{2,450},{3,451},{4,452},{5,453},{6,454},{7,455},{8... | collective-permute-start | bytes 208904 | tf_op jit(solution)/shard_map/ppermute | solution.py:283
  29.6 0.0 collective-permute-done.2.rest_2_
  29.6 0.0 copy-start.2
  29.6 1.9 %collective-permute-start.6 = (bf16[2,512,128]{2,1,0:T(8,128)(2,1)S(1)}, bf16[2,512,128]{2,1,0:T(8,128)(2,1)}, u32[]{:S(2)}, u32[]{:S(2)}) collective-permute-start(bf16[2,512,128]{2,1,0:T(8,128)(2,1)S(1)} %get-tuple-element.51), channel_id=1, source_target_pairs={{0,6},{1,7},{2,4},{3,5},{4,2},{5,3},{6,0},{7,1},{8,14},{9,15},{10,... | collective-permute-start | bytes 786440 | tf_op jit(solution)/shard_map/ppermute | solution.py:283
  31.5 1.7 %collective-permute-done.1 = bf16[17,16,128]{2,1,0:T(8,128)(2,1)S(1)} collective-permute-done((bf16[17,16,128]{2,1,0:T(8,128)(2,1)S(1)}, bf16[17,16,128]{2,1,0:T(8,128)(2,1)S(1)}, u32[]{:S(2)}, u32[]{:S(2)}) %collective-permute-start.1) | collective-permute-done | bytes 69664 | tf_op jit(solution)/shard_map/ppermute | solution.py:283
  33.2 0.9 broadcast_select_fusion
  34.1 4.3 %all-to-all-start = ((bf16[8,17,16,128]{3,2,1,0:T(8,128)(2,1)}), bf16[8,17,16,128]{3,2,1,0:T(8,128)(2,1)S(1)}, u32[]{:S(2)}, u32[]{:S(2)}) async-start(bf16[8,17,16,128]{3,2,1,0:T(8,128)(2,1)} %broadcast_select_fusion), calls=%async_computation | async-start | bytes 1114112 | tf_op jit(solution)/shard_map/all_to_all | solution.py:289
  38.4 0.0 copy-start.5
  38.4 2.1 %copy.10 = bf16[16,256,2,128]{3,1,2,0:T(8,128)(2,1)S(1)} copy(bf16[16,256,2,128]{3,2,1,0:T(2,128)(2,1)} %param.9) | data formatting | bytes 4194304 | tf_op jit(solution)/shard_map/optimization_barrier | solution.py:315
  40.5 0.0 copy-done.2
  40.5 0.0 copy-done.5
  40.5 0.0 copy-start.4
  40.6 1.9 %collective-permute-start.7 = (bf16[2,512,128]{2,1,0:T(8,128)(2,1)S(1)}, bf16[2,512,128]{2,1,0:T(8,128)(2,1)}, u32[]{:S(2)}, u32[]{:S(2)}) collective-permute-start(bf16[2,512,128]{2,1,0:T(8,128)(2,1)S(1)} %get-tuple-element.54), channel_id=1, source_target_pairs={{0,7},{1,6},{2,5},{3,4},{4,3},{5,2},{6,1},{7,0},{8,15},{9,14},{10,... | collective-permute-start | bytes 786440 | tf_op jit(solution)/shard_map/ppermute | solution.py:283
  42.5 0.2 fusion.3.kv_ref
  42.7 0.0 copy-done.4
  42.7 1.2 %local_attention.1 = (f32[16,16,128]{2,1,0:T(8,128)S(1)}, f32[16,16,128]{2,1,0:T(8,128)S(1)}) custom-call(s32[16]{0:T(128)S(1)} %copy-done.4, bf16[16,16,128]{2,1,0:T(8,128)(2,1)S(1)} %reshape.51.q_ref, bf16[16,2,272,128]{3,2,1,0:T(8,128)(2,1)S(1)} %fusion.3.kv_ref), custom_call_target="tpu_custom_call" | custom-call | flops 20000000000 | bytes 2500000 | tf_op jit(solution)/shard_map/local_attention/pallas_call | solution.py:53
  43.9 0.0 collective-permute-done.3.rest_2_
  44.0 2.5 %collective-permute-start.4 = (bf16[2,2,512,128]{3,2,1,0:T(8,128)(2,1)S(1)}, bf16[2,2,512,128]{3,2,1,0:T(8,128)(2,1)S(1)}, u32[]{:S(2)}, u32[]{:S(2)}) collective-permute-start(bf16[2,2,512,128]{3,2,1,0:T(8,128)(2,1)S(1)} %collective-permute-done.3.rest_2_), channel_id=1, source_target_pairs={{0,1},{1,0},{2,3},{3,2},{4,5},{5,4},{6,7},{7,6},{8,9},{9,8},{10,11... | collective-permute-start | bytes 1572872 | tf_op jit(solution)/shard_map/ppermute | solution.py:283
  46.4 1.8 %all-to-all-done.q_ref = bf16[8,17,16,128]{3,2,1,0:T(8,128)(2,1)S(1)} async-done(((bf16[8,17,16,128]{3,2,1,0:T(8,128)(2,1)}), bf16[8,17,16,128]{3,2,1,0:T(8,128)(2,1)S(1)}, u32[]{:S(2)}, u32[]{:S(2)}) %all-to-all-start) | async-done | bytes 557088 | tf_op jit(solution)/shard_map/all_to_all | solution.py:289
  48.2 0.2 convert_reduce_fusion
  48.4 0.1 reshape.53
  48.5 1.5 %pack_queries.1 = (bf16[144,16,128]{2,1,0:T(8,128)(2,1)S(1)}, s32[130]{0:T(256)S(1)}) custom-call(s32[128]{0:T(128)S(1)} %and_convert_fusion.live_ref, bf16[8,17,16,128]{3,2,1,0:T(8,128)(2,1)S(1)} %all-to-all-done.q_ref), custom_call_target="tpu_custom_call" | custom-call | tf_op jit(solution)/shard_map/pack_queries/pallas_call | solution.py:102
  50.0 0.0 copy-start.3
  50.1 0.9 %copy-done.3 = bf16[2,512,128]{2,1,0:T(8,128)(2,1)S(1)} copy-done((bf16[2,512,128]{2,1,0:T(8,128)(2,1)S(1)}, bf16[2,512,128]{2,1,0:T(8,128)(2,1)}, u32[]{:S(2)}) %copy-start.3) | copy-done | bytes 262168
  51.0 1.4 %attend_stage.2 = (f32[8,256,128]{2,1,0:T(8,128)S(1)}, f32[8,256,128]{2,1,0:T(8,128)S(1)}) custom-call(s32[130]{0:T(256)S(1)} %get-tuple-element.42.index, bf16[144,16,128]{2,1,0:T(8,128)(2,1)S(1)} %get-tuple-element.43.packed, bf16[2,512,128]{2,1,0:T(8,128)(2,1)S(1)} %get-tuple-element.44.rest_0_, bf16[2,512,128]{2,1,0:T(8,128)(2,1)S(1)} %collective-permute-done.rest_1_, ...), custom_call_target="tpu_custom_call" | custom-call | flops 10000000000 | bytes 2000000 | tf_op jit(solution)/shard_map/attend_stage/pallas_call | solution.py:145
  52.4 0.0 collective-permute-done.5.rest_4_
  52.5 0.0 collective-permute-done.6.rest_5_
  52.5 0.0 collective-permute-done.4.rest_3_
  52.5 2.1 %attend_stage.3 = (f32[8,256,128]{2,1,0:T(8,128)S(1)}, f32[8,256,128]{2,1,0:T(8,128)S(1)}) custom-call(s32[130]{0:T(256)S(1)} %get-tuple-element.42.index, bf16[144,16,128]{2,1,0:T(8,128)(2,1)S(1)} %get-tuple-element.43.packed, f32[8,256,128]{2,1,0:T(8,128)S(1)} %get-tuple-element.47.rest_0_, f32[8,256,128]{2,1,0:T(8,128)S(1)} %get-tuple-element.48.rest_1_, ...), custom_call_target="tpu_custom_call" | custom-call | flops 10000000000 | bytes 2000000 | tf_op jit(solution)/shard_map/attend_stage/pallas_call | solution.py:145
  54.6 2.2 %collective-permute-done.7.rest_0_ = bf16[2,512,128]{2,1,0:T(8,128)(2,1)} collective-permute-done((bf16[2,512,128]{2,1,0:T(8,128)(2,1)S(1)}, bf16[2,512,128]{2,1,0:T(8,128)(2,1)}, u32[]{:S(2)}, u32[]{:S(2)}) %collective-permute-start.7) | collective-permute-done | bytes 262176 | tf_op jit(solution)/shard_map/ppermute | solution.py:283
  56.9 1.6 %attend_late.1 = bf16[8,17,16,128]{3,2,1,0:T(8,128)(2,1)S(1)} custom-call(s32[130]{0:T(256)S(1)} %get-tuple-element.42.index, bf16[144,16,128]{2,1,0:T(8,128)(2,1)S(1)} %get-tuple-element.43.packed, f32[8,256,128]{2,1,0:T(8,128)S(1)} %get-tuple-element.52.attended_ref, f32[8,256,128]{2,1,0:T(8,128)S(1)} %get-tuple-element.53.level_ref, ...), custom_call_target="tpu_custom_call" | custom-call | flops 10000000000 | bytes 4000000 | tf_op jit(solution)/shard_map/attend_late/pallas_call | solution.py:199
  58.5 15.5 %all_to_all.10 = bf16[8,17,16,128]{3,2,1,0:T(8,128)(2,1)S(1)} all-to-all(bf16[8,17,16,128]{3,2,1,0:T(8,128)(2,1)S(1)} %attend_late.1), channel_id=1, replica_groups={{0,8,16,24,32,40,48,56},{64,72,80,88,96,104,112,120},{128,136,144,152,1..., dimensions={0} | all-to-all | bytes 1114112 | tf_op jit(solution)/shard_map/all_to_all | solution.py:289
  73.9 0.3 select_reduce_fusion
  74.2 3.7 %collective-permute-start.8 = (bf16[17,16,128]{2,1,0:T(8,128)(2,1)S(1)}, bf16[17,16,128]{2,1,0:T(8,128)(2,1)S(1)}, u32[]{:S(2)}, u32[]{:S(2)}) collective-permute-start(bf16[17,16,128]{2,1,0:T(8,128)(2,1)S(1)} %get-tuple-element.57), channel_id=1, source_target_pairs={{0,64},{1,65},{2,66},{3,67},{4,68},{5,69},{6,70},{7,71},{8,72},{9,... | collective-permute-start | bytes 208904 | tf_op jit(solution)/shard_map/ppermute | solution.py:283
  77.9 14.7 %collective-permute-done.8.refs_1_ = bf16[17,16,128]{2,1,0:T(8,128)(2,1)S(1)} collective-permute-done((bf16[17,16,128]{2,1,0:T(8,128)(2,1)S(1)}, bf16[17,16,128]{2,1,0:T(8,128)(2,1)S(1)}, u32[]{:S(2)}, u32[]{:S(2)}) %collective-permute-start.8) | collective-permute-done | bytes 69664 | tf_op jit(solution)/shard_map/ppermute | solution.py:283
  92.6 0.1 merge_parts.1
  92.8 0.7 reshape.52
  (7 shorter events, 0.1 us)
Async XLA Ops:
  0.0 15.8 %copy-start = (s32[64]{0:T(128)S(1)}, s32[64]{0:T(128)}, u32[]{:S(2)}) copy-start(s32[64]{0:T(128)} %param.11) | copy-start | bytes 772
  0.0 1.6 %copy-start.1 = (bf16[1,512,2,8,128]{4,3,2,1,0:T(8,128)(2,1)S(1)}, bf16[1,512,2,8,128]{4,3,2,1,0:T(8,128)(2,1)}, u32[]{:S(2)}) copy-start(bf16[1,512,2,8,128]{4,3,2,1,0:T(8,128)(2,1)} %param.10) | copy-start | bytes 6291460
  2.6 15.0 %collective-permute-start = (bf16[2,512,128]{2,1,0:T(8,128)(2,1)S(1)}, bf16[2,512,128]{2,1,0:T(8,128)(2,1)S(1)}, u32[]{:S(2)}, u32[]{:S(2)}) collective-permute-start(bf16[2,512,128]{2,1,0:T(8,128)(2,1)S(1)} %get-tuple-element.31), channel_id=1, source_target_pairs={{0,1},{1,0},{2,3},{3,2},{4,5},{5,4},{6,7},{7,6},{8,9},{9,8},{10,11... | collective-permute-start | bytes 786440 | tf_op jit(solution)/shard_map/ppermute | solution.py:283
  4.5 25.0 %collective-permute-start.2 = (bf16[2,512,128]{2,1,0:T(8,128)(2,1)S(1)}, bf16[2,512,128]{2,1,0:T(8,128)(2,1)S(1)}, u32[]{:S(2)}, u32[]{:S(2)}) collective-permute-start(bf16[2,512,128]{2,1,0:T(8,128)(2,1)S(1)} %get-tuple-element.34), channel_id=1, source_target_pairs={{0,4},{1,5},{2,6},{3,7},{4,0},{5,1},{6,2},{7,3},{8,12},{9,13},{10,... | collective-permute-start | bytes 786440 | tf_op jit(solution)/shard_map/ppermute | solution.py:283
  10.5 33.4 %collective-permute-start.3 = (bf16[2,2,512,128]{3,2,1,0:T(8,128)(2,1)S(1)}, bf16[2,2,512,128]{3,2,1,0:T(8,128)(2,1)S(1)}, u32[]{:S(2)}, u32[]{:S(2)}) collective-permute-start(bf16[2,2,512,128]{3,2,1,0:T(8,128)(2,1)S(1)} %get-tuple-element.49), channel_id=1, source_target_pairs={{0,2},{1,3},{2,0},{3,1},{4,6},{5,7},{6,4},{7,5},{8,10},{9,11},{10,... | collective-permute-start | bytes 1572872 | tf_op jit(solution)/shard_map/ppermute | solution.py:283
  12.5 40.0 %collective-permute-start.5 = (bf16[2,512,128]{2,1,0:T(8,128)(2,1)S(1)}, bf16[2,512,128]{2,1,0:T(8,128)(2,1)S(1)}, u32[]{:S(2)}, u32[]{:S(2)}) collective-permute-start(bf16[2,512,128]{2,1,0:T(8,128)(2,1)S(1)} %get-tuple-element.50), channel_id=1, source_target_pairs={{0,5},{1,4},{2,7},{3,6},{4,1},{5,0},{6,3},{7,2},{8,13},{9,12},{10,... | collective-permute-start | bytes 786440 | tf_op jit(solution)/shard_map/ppermute | solution.py:283
  17.6 15.6 %collective-permute-start.1 = (bf16[17,16,128]{2,1,0:T(8,128)(2,1)S(1)}, bf16[17,16,128]{2,1,0:T(8,128)(2,1)S(1)}, u32[]{:S(2)}, u32[]{:S(2)}) collective-permute-start(bf16[17,16,128]{2,1,0:T(8,128)(2,1)S(1)} %pad_maximum_fusion), channel_id=1, source_target_pairs={{0,448},{1,449},{2,450},{3,451},{4,452},{5,453},{6,454},{7,455},{8... | collective-permute-start | bytes 208904 | tf_op jit(solution)/shard_map/ppermute | solution.py:283
  29.6 10.9 %copy-start.2 = (bf16[2,512,128]{2,1,0:T(8,128)(2,1)}, bf16[2,512,128]{2,1,0:T(8,128)(2,1)S(1)}, u32[]{:S(2)}) copy-start(bf16[2,512,128]{2,1,0:T(8,128)(2,1)S(1)} %collective-permute-done.2.rest_2_) | copy-start | bytes 786436
  29.6 22.9 %collective-permute-start.6 = (bf16[2,512,128]{2,1,0:T(8,128)(2,1)S(1)}, bf16[2,512,128]{2,1,0:T(8,128)(2,1)}, u32[]{:S(2)}, u32[]{:S(2)}) collective-permute-start(bf16[2,512,128]{2,1,0:T(8,128)(2,1)S(1)} %get-tuple-element.51), channel_id=1, source_target_pairs={{0,6},{1,7},{2,4},{3,5},{4,2},{5,3},{6,0},{7,1},{8,14},{9,15},{10,... | collective-permute-start | bytes 786440 | tf_op jit(solution)/shard_map/ppermute | solution.py:283
  34.1 14.1 %all-to-all-start = ((bf16[8,17,16,128]{3,2,1,0:T(8,128)(2,1)}), bf16[8,17,16,128]{3,2,1,0:T(8,128)(2,1)S(1)}, u32[]{:S(2)}, u32[]{:S(2)}) async-start(bf16[8,17,16,128]{3,2,1,0:T(8,128)(2,1)} %broadcast_select_fusion), calls=%async_computation | async-start | bytes 1114112 | tf_op jit(solution)/shard_map/all_to_all | solution.py:289
  38.4 2.1 %copy-start.5 = (bf16[16,2,2,128]{3,2,1,0:T(2,128)(2,1)S(1)}, bf16[16,2,2,128]{3,2,1,0:T(2,128)(2,1)}, u32[]{:S(2)}) copy-start(bf16[16,2,2,128]{3,2,1,0:T(2,128)(2,1)} %param.8) | copy-start | bytes 49156
  40.5 2.2 %copy-start.4 = (s32[16]{0:T(128)S(1)}, s32[16]{0:T(128)}, u32[]{:S(2)}) copy-start(s32[16]{0:T(128)} %len_ref.1) | copy-start | bytes 196
  40.6 16.3 %collective-permute-start.7 = (bf16[2,512,128]{2,1,0:T(8,128)(2,1)S(1)}, bf16[2,512,128]{2,1,0:T(8,128)(2,1)}, u32[]{:S(2)}, u32[]{:S(2)}) collective-permute-start(bf16[2,512,128]{2,1,0:T(8,128)(2,1)S(1)} %get-tuple-element.54), channel_id=1, source_target_pairs={{0,7},{1,6},{2,5},{3,4},{4,3},{5,2},{6,1},{7,0},{8,15},{9,14},{10,... | collective-permute-start | bytes 786440 | tf_op jit(solution)/shard_map/ppermute | solution.py:283
  44.0 8.5 %collective-permute-start.4 = (bf16[2,2,512,128]{3,2,1,0:T(8,128)(2,1)S(1)}, bf16[2,2,512,128]{3,2,1,0:T(8,128)(2,1)S(1)}, u32[]{:S(2)}, u32[]{:S(2)}) collective-permute-start(bf16[2,2,512,128]{3,2,1,0:T(8,128)(2,1)S(1)} %collective-permute-done.3.rest_2_), channel_id=1, source_target_pairs={{0,1},{1,0},{2,3},{3,2},{4,5},{5,4},{6,7},{7,6},{8,9},{9,8},{10,11... | collective-permute-start | bytes 1572872 | tf_op jit(solution)/shard_map/ppermute | solution.py:283
  50.0 1.0 %copy-start.3 = (bf16[2,512,128]{2,1,0:T(8,128)(2,1)S(1)}, bf16[2,512,128]{2,1,0:T(8,128)(2,1)}, u32[]{:S(2)}) copy-start(bf16[2,512,128]{2,1,0:T(8,128)(2,1)} %copy-done.2) | copy-start | bytes 786436
  74.2 18.4 %collective-permute-start.8 = (bf16[17,16,128]{2,1,0:T(8,128)(2,1)S(1)}, bf16[17,16,128]{2,1,0:T(8,128)(2,1)S(1)}, u32[]{:S(2)}, u32[]{:S(2)}) collective-permute-start(bf16[17,16,128]{2,1,0:T(8,128)(2,1)S(1)} %get-tuple-element.57), channel_id=1, source_target_pairs={{0,64},{1,65},{2,66},{3,67},{4,68},{5,69},{6,70},{7,71},{8,72},{9,... | collective-permute-start | bytes 208904 | tf_op jit(solution)/shard_map/ppermute | solution.py:283

commit v4 on v3

--- a/solution.py
+++ b/solution.py
@@ -11,7 +11,7 @@
 WINDOW = 8
 DRAFT = 2
 BLOCK_ROWS = 16
-FLIPS = ((0,), (1,), (2, 3), (4,), (5,), (6,), (7,))
+FLIPS = ((0,), (1,), (2, 3), (6,), (7,), (4,), (5,))
 STAGE_FLOPS = 10_000_000_000
 LOCAL_FLOPS = 20_000_000_000
 VMEM_BYTES = 16 * 1024 * 1024
@@ -304,7 +304,7 @@
     sent = jnp.concatenate([q, tag.reshape(1, vectors, head_dim)])
     own, beside, near, *far = split_prefix(lax.axis_index("tensor"), prefix_kv[0])
     beside, far[2], sent = lax.optimization_barrier((moved(beside, 0, 1), far[2], sent))
-    far[:3] = [moved(block, 0, 4 + step) for step, block in enumerate(far[:3])]
+    far[:3] = [moved(block, 0, flip) for flip, block in zip((6, 7, 4), far[:3])]
     near, after = moved(near, 0, 2), moved(sent, -WINDOW)
 
     mine = (cells < place)[:, None, None, None]
@@ -313,7 +313,7 @@
     tags = arrived[:, rows, :, 0].astype(jnp.int32)
     live = (tags > 0) & (tags == ((cells - place) % WINDOW)[:, None])
     own_kv, new_kv, far[3], cell = lax.optimization_barrier((own_kv, new_kv, far[3], cell))
-    far[3] = moved(far[3], 0, 7)
+    far[3] = moved(far[3], 0, 5)
     late_q, far[0] = lax.optimization_barrier((q, far[0]))
     local, local_lse = local_attention(late_q, own_kv, new_kv, own_len)
     arrived, local, local_lse = lax.optimization_barrier((arrived, local, local_lse))

time: 94.1 us -> 94.1 us (level)
  the two profiles are of different devices: /device:TPU:128 before, /device:TPU:1 now
where the time goes in v4:
time: 94.1 us; the launch traced here: 92.9 us
  starting transfers between devices  43.3 us (46%)
  waiting for transfers between devices  17.6 us (19%)
  blocking collectives  13.2 us (14%)
  Pallas kernels  9.06 us (10%)
  local copies, waits for them, and re-layouts  7.17 us (8%)
  other arithmetic  2.3 us (2%)
    ppermute x9, starting transfers between devices, moved(): return lax.ppermute(x, ('group', 'tensor'), pairs)  39.2 us
    ppermute x9, waiting for transfers between devices, moved(): return lax.ppermute(x, ('group', 'tensor'), pairs)  17.6 us
    all_to_all x1, blocking collectives, windowed(): lax.all_to_all(x, 'group', 0, 0, axis_index_groups=windows, tiled=True)  13.2 us
    all_to_all x1, starting transfers between devices, windowed(): lax.all_to_all(x, 'group', 0, 0, axis_index_groups=windows, tiled=True)  4.13 us
    pallas_call x2, Pallas kernels, attend_stage(): pl.pallas_call(functools.partial(stage_kernel, len(state) // 2, halves),...  3.56 us
    unnamed x12, local copies, waits for them, and re-layouts  2.57 us
    optimization_barrier x2, local copies, waits for them, and re-layouts, on_device(): lax.optimization_barrier((own_kv, new_kv, far[3], cell))  2.11 us
  transfers between devices with their start and end apart: 10, of which 3 were waited for; matrix products, arithmetic and copies ran while one was open for 6% of the time, Pallas kernels for 7%

profile of v4, /device:TPU:1, one launch (start us, length us, event | category | flops | bytes accessed | tf_op | source)
XLA Modules:
  0.0 92.9 jit_solution(1044590117785259403)
XLA Ops:
  0.0 0.0 copy-start
  0.0 0.0 copy-start.1
  0.0 1.6 %copy-done.1 = bf16[1,512,2,8,128]{4,3,2,1,0:T(8,128)(2,1)S(1)} copy-done((bf16[1,512,2,8,128]{4,3,2,1,0:T(8,128)(2,1)S(1)}, bf16[1,512,2,8,128]{4,3,2,1,0:T(8,128)(2,1)}, u32[]{:S(2)}) %copy-start.1) | copy-done | bytes 2097176
  1.6 1.0 %split_prefix.1 = (bf16[2,512,128]{2,1,0:T(8,128)(2,1)S(1)}, bf16[2,512,128]{2,1,0:T(8,128)(2,1)S(1)}, bf16[2,2,512,128]{3,2,1,0:T(8,128)(2,1)S(1)}, bf16[2,512,...) custom-call(s32[1]{0:T(128)} %bitcast.lane_ref, ...), custom_call_target="tpu_custom_call" | custom-call | bytes 4194304 | tf_op jit(solution)/shard_map/split_prefix/pallas_call | solution.py:263
  2.6 8.8 %collective-permute-start = (bf16[2,512,128]{2,1,0:T(8,128)(2,1)S(1)}, bf16[2,512,128]{2,1,0:T(8,128)(2,1)S(1)}, u32[]{:S(2)}, u32[]{:S(2)}) collective-permute-start(bf16[2,512,128]{2,1,0:T(8,128)(2,1)S(1)} %get-tuple-element.31), channel_id=1, source_target_pairs={{0,1},{1,0},{2,3},{3,2},{4,5},{5,4},{6,7},{7,6},{8,9},{9,8},{10,11... | collective-permute-start | bytes 786440 | tf_op jit(solution)/shard_map/ppermute | solution.py:283
  11.4 2.2 %collective-permute-start.2 = (bf16[2,512,128]{2,1,0:T(8,128)(2,1)S(1)}, bf16[2,512,128]{2,1,0:T(8,128)(2,1)S(1)}, u32[]{:S(2)}, u32[]{:S(2)}) collective-permute-start(bf16[2,512,128]{2,1,0:T(8,128)(2,1)S(1)} %get-tuple-element.34), channel_id=1, source_target_pairs={{0,6},{1,7},{2,4},{3,5},{4,2},{5,3},{6,0},{7,1},{8,14},{9,15},{10,... | collective-permute-start | bytes 786440 | tf_op jit(solution)/shard_map/ppermute | solution.py:283
  13.6 1.9 %collective-permute-start.3 = (bf16[2,2,512,128]{3,2,1,0:T(8,128)(2,1)S(1)}, bf16[2,2,512,128]{3,2,1,0:T(8,128)(2,1)S(1)}, u32[]{:S(2)}, u32[]{:S(2)}) collective-permute-start(bf16[2,2,512,128]{3,2,1,0:T(8,128)(2,1)S(1)} %get-tuple-element.49), channel_id=1, source_target_pairs={{0,2},{1,3},{2,0},{3,1},{4,6},{5,7},{6,4},{7,5},{8,10},{9,11},{10,... | collective-permute-start | bytes 1572872 | tf_op jit(solution)/shard_map/ppermute | solution.py:283
  15.6 5.0 %collective-permute-start.5 = (bf16[2,512,128]{2,1,0:T(8,128)(2,1)S(1)}, bf16[2,512,128]{2,1,0:T(8,128)(2,1)S(1)}, u32[]{:S(2)}, u32[]{:S(2)}) collective-permute-start(bf16[2,512,128]{2,1,0:T(8,128)(2,1)S(1)} %get-tuple-element.50), channel_id=1, source_target_pairs={{0,7},{1,6},{2,5},{3,4},{4,3},{5,2},{6,1},{7,0},{8,15},{9,14},{10,... | collective-permute-start | bytes 786440 | tf_op jit(solution)/shard_map/ppermute | solution.py:283
  20.6 0.7 compare_select_fusion
  21.3 0.0 copy-done
  21.3 0.7 gather_fusion
  22.0 0.9 reshape.51.q_ref
  22.9 0.1 eq.17
  22.9 0.1 eq.18
  23.0 0.1 broadcast_in_dim.47
  23.1 0.0 collective-permute-done.rest_1_
  23.1 9.5 %collective-permute-start.1 = (bf16[17,16,128]{2,1,0:T(8,128)(2,1)S(1)}, bf16[17,16,128]{2,1,0:T(8,128)(2,1)S(1)}, u32[]{:S(2)}, u32[]{:S(2)}) collective-permute-start(bf16[17,16,128]{2,1,0:T(8,128)(2,1)S(1)} %pad_maximum_fusion), channel_id=1, source_target_pairs={{0,448},{1,449},{2,450},{3,451},{4,452},{5,453},{6,454},{7,455},{8... | collective-permute-start | bytes 208904 | tf_op jit(solution)/shard_map/ppermute | solution.py:283
  32.6 0.0 collective-permute-done.2.rest_2_
  32.7 0.0 copy-start.2
  32.7 4.0 %collective-permute-start.6 = (bf16[2,512,128]{2,1,0:T(8,128)(2,1)S(1)}, bf16[2,512,128]{2,1,0:T(8,128)(2,1)}, u32[]{:S(2)}, u32[]{:S(2)}) collective-permute-start(bf16[2,512,128]{2,1,0:T(8,128)(2,1)S(1)} %get-tuple-element.51), channel_id=1, source_target_pairs={{0,4},{1,5},{2,6},{3,7},{4,0},{5,1},{6,2},{7,3},{8,12},{9,13},{10,... | collective-permute-start | bytes 786440 | tf_op jit(solution)/shard_map/ppermute | solution.py:283
  36.7 0.0 collective-permute-done.1
  36.7 0.9 broadcast_select_fusion
  37.6 4.1 %all-to-all-start = ((bf16[8,17,16,128]{3,2,1,0:T(8,128)(2,1)}), bf16[8,17,16,128]{3,2,1,0:T(8,128)(2,1)S(1)}, u32[]{:S(2)}, u32[]{:S(2)}) async-start(bf16[8,17,16,128]{3,2,1,0:T(8,128)(2,1)} %broadcast_select_fusion), calls=%async_computation | async-start | bytes 1114112 | tf_op jit(solution)/shard_map/all_to_all | solution.py:289
  41.7 0.0 copy-start.5
  41.7 2.1 %copy.10 = bf16[16,256,2,128]{3,1,2,0:T(8,128)(2,1)S(1)} copy(bf16[16,256,2,128]{3,2,1,0:T(2,128)(2,1)} %param.9) | data formatting | bytes 4194304 | tf_op jit(solution)/shard_map/optimization_barrier | solution.py:315
  43.8 0.0 copy-done.2
  43.9 0.0 copy-done.5
  43.9 0.0 copy-start.4
  43.9 3.9 %collective-permute-start.7 = (bf16[2,512,128]{2,1,0:T(8,128)(2,1)S(1)}, bf16[2,512,128]{2,1,0:T(8,128)(2,1)}, u32[]{:S(2)}, u32[]{:S(2)}) collective-permute-start(bf16[2,512,128]{2,1,0:T(8,128)(2,1)S(1)} %get-tuple-element.54), channel_id=1, source_target_pairs={{0,5},{1,4},{2,7},{3,6},{4,1},{5,0},{6,3},{7,2},{8,13},{9,12},{10,... | collective-permute-start | bytes 786440 | tf_op jit(solution)/shard_map/ppermute | solution.py:283
  47.8 0.2 fusion.3.kv_ref
  48.0 0.0 copy-done.4
  48.0 1.2 %local_attention.1 = (f32[16,16,128]{2,1,0:T(8,128)S(1)}, f32[16,16,128]{2,1,0:T(8,128)S(1)}) custom-call(s32[16]{0:T(128)S(1)} %copy-done.4, bf16[16,16,128]{2,1,0:T(8,128)(2,1)S(1)} %reshape.51.q_ref, bf16[16,2,272,128]{3,2,1,0:T(8,128)(2,1)S(1)} %fusion.3.kv_ref), custom_call_target="tpu_custom_call" | custom-call | flops 20000000000 | bytes 2500000 | tf_op jit(solution)/shard_map/local_attention/pallas_call | solution.py:53
  49.2 0.0 collective-permute-done.3.rest_2_
  49.2 1.9 %collective-permute-start.4 = (bf16[2,2,512,128]{3,2,1,0:T(8,128)(2,1)S(1)}, bf16[2,2,512,128]{3,2,1,0:T(8,128)(2,1)S(1)}, u32[]{:S(2)}, u32[]{:S(2)}) collective-permute-start(bf16[2,2,512,128]{3,2,1,0:T(8,128)(2,1)S(1)} %collective-permute-done.3.rest_2_), channel_id=1, source_target_pairs={{0,1},{1,0},{2,3},{3,2},{4,5},{5,4},{6,7},{7,6},{8,9},{9,8},{10,11... | collective-permute-start | bytes 1572872 | tf_op jit(solution)/shard_map/ppermute | solution.py:283
  51.2 0.0 all-to-all-done.q_ref
  51.2 0.2 convert_reduce_fusion
  51.4 0.1 reshape.53
  51.5 1.5 %pack_queries.1 = (bf16[144,16,128]{2,1,0:T(8,128)(2,1)S(1)}, s32[130]{0:T(256)S(1)}) custom-call(s32[128]{0:T(128)S(1)} %and_convert_fusion.live_ref, bf16[8,17,16,128]{3,2,1,0:T(8,128)(2,1)S(1)} %all-to-all-done.q_ref), custom_call_target="tpu_custom_call" | custom-call | tf_op jit(solution)/shard_map/pack_queries/pallas_call | solution.py:102
  53.0 0.0 copy-start.3
  53.0 0.9 %copy-done.3 = bf16[2,512,128]{2,1,0:T(8,128)(2,1)S(1)} copy-done((bf16[2,512,128]{2,1,0:T(8,128)(2,1)S(1)}, bf16[2,512,128]{2,1,0:T(8,128)(2,1)}, u32[]{:S(2)}) %copy-start.3) | copy-done | bytes 262168
  53.9 1.4 %attend_stage.2 = (f32[8,256,128]{2,1,0:T(8,128)S(1)}, f32[8,256,128]{2,1,0:T(8,128)S(1)}) custom-call(s32[130]{0:T(256)S(1)} %get-tuple-element.42.index, bf16[144,16,128]{2,1,0:T(8,128)(2,1)S(1)} %get-tuple-element.43.packed, bf16[2,512,128]{2,1,0:T(8,128)(2,1)S(1)} %get-tuple-element.44.rest_0_, bf16[2,512,128]{2,1,0:T(8,128)(2,1)S(1)} %collective-permute-done.rest_1_, ...), custom_call_target="tpu_custom_call" | custom-call | flops 10000000000 | bytes 2000000 | tf_op jit(solution)/shard_map/attend_stage/pallas_call | solution.py:145
  55.4 0.0 collective-permute-done.5.rest_4_
  55.4 1.8 %collective-permute-done.6.rest_5_ = bf16[2,512,128]{2,1,0:T(8,128)(2,1)} collective-permute-done((bf16[2,512,128]{2,1,0:T(8,128)(2,1)S(1)}, bf16[2,512,128]{2,1,0:T(8,128)(2,1)}, u32[]{:S(2)}, u32[]{:S(2)}) %collective-permute-start.6) | collective-permute-done | bytes 262176 | tf_op jit(solution)/shard_map/ppermute | solution.py:283
  57.2 0.0 collective-permute-done.4.rest_3_
  57.2 2.1 %attend_stage.3 = (f32[8,256,128]{2,1,0:T(8,128)S(1)}, f32[8,256,128]{2,1,0:T(8,128)S(1)}) custom-call(s32[130]{0:T(256)S(1)} %get-tuple-element.42.index, bf16[144,16,128]{2,1,0:T(8,128)(2,1)S(1)} %get-tuple-element.43.packed, f32[8,256,128]{2,1,0:T(8,128)S(1)} %get-tuple-element.47.rest_0_, f32[8,256,128]{2,1,0:T(8,128)S(1)} %get-tuple-element.48.rest_1_, ...), custom_call_target="tpu_custom_call" | custom-call | flops 10000000000 | bytes 2000000 | tf_op jit(solution)/shard_map/attend_stage/pallas_call | solution.py:145
  59.4 3.5 %collective-permute-done.7.rest_0_ = bf16[2,512,128]{2,1,0:T(8,128)(2,1)} collective-permute-done((bf16[2,512,128]{2,1,0:T(8,128)(2,1)S(1)}, bf16[2,512,128]{2,1,0:T(8,128)(2,1)}, u32[]{:S(2)}, u32[]{:S(2)}) %collective-permute-start.7) | collective-permute-done | bytes 262176 | tf_op jit(solution)/shard_map/ppermute | solution.py:283
  62.9 1.6 %attend_late.1 = bf16[8,17,16,128]{3,2,1,0:T(8,128)(2,1)S(1)} custom-call(s32[130]{0:T(256)S(1)} %get-tuple-element.42.index, bf16[144,16,128]{2,1,0:T(8,128)(2,1)S(1)} %get-tuple-element.43.packed, f32[8,256,128]{2,1,0:T(8,128)S(1)} %get-tuple-element.52.attended_ref, f32[8,256,128]{2,1,0:T(8,128)S(1)} %get-tuple-element.53.level_ref, ...), custom_call_target="tpu_custom_call" | custom-call | flops 10000000000 | bytes 4000000 | tf_op jit(solution)/shard_map/attend_late/pallas_call | solution.py:199
  64.5 13.2 %all_to_all.10 = bf16[8,17,16,128]{3,2,1,0:T(8,128)(2,1)S(1)} all-to-all(bf16[8,17,16,128]{3,2,1,0:T(8,128)(2,1)S(1)} %attend_late.1), channel_id=1, replica_groups={{0,8,16,24,32,40,48,56},{64,72,80,88,96,104,112,120},{128,136,144,152,1..., dimensions={0} | all-to-all | bytes 1114112 | tf_op jit(solution)/shard_map/all_to_all | solution.py:289
  77.7 0.3 select_reduce_fusion
  77.9 1.9 %collective-permute-start.8 = (bf16[17,16,128]{2,1,0:T(8,128)(2,1)S(1)}, bf16[17,16,128]{2,1,0:T(8,128)(2,1)S(1)}, u32[]{:S(2)}, u32[]{:S(2)}) collective-permute-start(bf16[17,16,128]{2,1,0:T(8,128)(2,1)S(1)} %get-tuple-element.57), channel_id=1, source_target_pairs={{0,64},{1,65},{2,66},{3,67},{4,68},{5,69},{6,70},{7,71},{8,72},{9,... | collective-permute-start | bytes 208904 | tf_op jit(solution)/shard_map/ppermute | solution.py:283
  79.9 12.3 %collective-permute-done.8.refs_1_ = bf16[17,16,128]{2,1,0:T(8,128)(2,1)S(1)} collective-permute-done((bf16[17,16,128]{2,1,0:T(8,128)(2,1)S(1)}, bf16[17,16,128]{2,1,0:T(8,128)(2,1)S(1)}, u32[]{:S(2)}, u32[]{:S(2)}) %collective-permute-start.8) | collective-permute-done | bytes 69664 | tf_op jit(solution)/shard_map/ppermute | solution.py:283
  92.1 0.1 merge_parts.1
  92.3 0.7 reshape.52
  (7 shorter events, 0.1 us)
Async XLA Ops:
  0.0 21.3 %copy-start = (s32[64]{0:T(128)S(1)}, s32[64]{0:T(128)}, u32[]{:S(2)}) copy-start(s32[64]{0:T(128)} %param.11) | copy-start | bytes 772
  0.0 1.6 %copy-start.1 = (bf16[1,512,2,8,128]{4,3,2,1,0:T(8,128)(2,1)S(1)}, bf16[1,512,2,8,128]{4,3,2,1,0:T(8,128)(2,1)}, u32[]{:S(2)}) copy-start(bf16[1,512,2,8,128]{4,3,2,1,0:T(8,128)(2,1)} %param.10) | copy-start | bytes 6291460
  2.6 20.5 %collective-permute-start = (bf16[2,512,128]{2,1,0:T(8,128)(2,1)S(1)}, bf16[2,512,128]{2,1,0:T(8,128)(2,1)S(1)}, u32[]{:S(2)}, u32[]{:S(2)}) collective-permute-start(bf16[2,512,128]{2,1,0:T(8,128)(2,1)S(1)} %get-tuple-element.31), channel_id=1, source_target_pairs={{0,1},{1,0},{2,3},{3,2},{4,5},{5,4},{6,7},{7,6},{8,9},{9,8},{10,11... | collective-permute-start | bytes 786440 | tf_op jit(solution)/shard_map/ppermute | solution.py:283
  11.4 21.3 %collective-permute-start.2 = (bf16[2,512,128]{2,1,0:T(8,128)(2,1)S(1)}, bf16[2,512,128]{2,1,0:T(8,128)(2,1)S(1)}, u32[]{:S(2)}, u32[]{:S(2)}) collective-permute-start(bf16[2,512,128]{2,1,0:T(8,128)(2,1)S(1)} %get-tuple-element.34), channel_id=1, source_target_pairs={{0,6},{1,7},{2,4},{3,5},{4,2},{5,3},{6,0},{7,1},{8,14},{9,15},{10,... | collective-permute-start | bytes 786440 | tf_op jit(solution)/shard_map/ppermute | solution.py:283
  13.6 35.6 %collective-permute-start.3 = (bf16[2,2,512,128]{3,2,1,0:T(8,128)(2,1)S(1)}, bf16[2,2,512,128]{3,2,1,0:T(8,128)(2,1)S(1)}, u32[]{:S(2)}, u32[]{:S(2)}) collective-permute-start(bf16[2,2,512,128]{3,2,1,0:T(8,128)(2,1)S(1)} %get-tuple-element.49), channel_id=1, source_target_pairs={{0,2},{1,3},{2,0},{3,1},{4,6},{5,7},{6,4},{7,5},{8,10},{9,11},{10,... | collective-permute-start | bytes 1572872 | tf_op jit(solution)/shard_map/ppermute | solution.py:283
  15.6 39.8 %collective-permute-start.5 = (bf16[2,512,128]{2,1,0:T(8,128)(2,1)S(1)}, bf16[2,512,128]{2,1,0:T(8,128)(2,1)S(1)}, u32[]{:S(2)}, u32[]{:S(2)}) collective-permute-start(bf16[2,512,128]{2,1,0:T(8,128)(2,1)S(1)} %get-tuple-element.50), channel_id=1, source_target_pairs={{0,7},{1,6},{2,5},{3,4},{4,3},{5,2},{6,1},{7,0},{8,15},{9,14},{10,... | collective-permute-start | bytes 786440 | tf_op jit(solution)/shard_map/ppermute | solution.py:283
  23.1 13.6 %collective-permute-start.1 = (bf16[17,16,128]{2,1,0:T(8,128)(2,1)S(1)}, bf16[17,16,128]{2,1,0:T(8,128)(2,1)S(1)}, u32[]{:S(2)}, u32[]{:S(2)}) collective-permute-start(bf16[17,16,128]{2,1,0:T(8,128)(2,1)S(1)} %pad_maximum_fusion), channel_id=1, source_target_pairs={{0,448},{1,449},{2,450},{3,451},{4,452},{5,453},{6,454},{7,455},{8... | collective-permute-start | bytes 208904 | tf_op jit(solution)/shard_map/ppermute | solution.py:283
  32.7 11.2 %copy-start.2 = (bf16[2,512,128]{2,1,0:T(8,128)(2,1)}, bf16[2,512,128]{2,1,0:T(8,128)(2,1)S(1)}, u32[]{:S(2)}) copy-start(bf16[2,512,128]{2,1,0:T(8,128)(2,1)S(1)} %collective-permute-done.2.rest_2_) | copy-start | bytes 786436
  32.7 24.6 %collective-permute-start.6 = (bf16[2,512,128]{2,1,0:T(8,128)(2,1)S(1)}, bf16[2,512,128]{2,1,0:T(8,128)(2,1)}, u32[]{:S(2)}, u32[]{:S(2)}) collective-permute-start(bf16[2,512,128]{2,1,0:T(8,128)(2,1)S(1)} %get-tuple-element.51), channel_id=1, source_target_pairs={{0,4},{1,5},{2,6},{3,7},{4,0},{5,1},{6,2},{7,3},{8,12},{9,13},{10,... | collective-permute-start | bytes 786440 | tf_op jit(solution)/shard_map/ppermute | solution.py:283
  37.6 13.6 %all-to-all-start = ((bf16[8,17,16,128]{3,2,1,0:T(8,128)(2,1)}), bf16[8,17,16,128]{3,2,1,0:T(8,128)(2,1)S(1)}, u32[]{:S(2)}, u32[]{:S(2)}) async-start(bf16[8,17,16,128]{3,2,1,0:T(8,128)(2,1)} %broadcast_select_fusion), calls=%async_computation | async-start | bytes 1114112 | tf_op jit(solution)/shard_map/all_to_all | solution.py:289
  41.7 2.1 %copy-start.5 = (bf16[16,2,2,128]{3,2,1,0:T(2,128)(2,1)S(1)}, bf16[16,2,2,128]{3,2,1,0:T(2,128)(2,1)}, u32[]{:S(2)}) copy-start(bf16[16,2,2,128]{3,2,1,0:T(2,128)(2,1)} %param.8) | copy-start | bytes 49156
  43.9 4.1 %copy-start.4 = (s32[16]{0:T(128)S(1)}, s32[16]{0:T(128)}, u32[]{:S(2)}) copy-start(s32[16]{0:T(128)} %len_ref.1) | copy-start | bytes 196
  43.9 19.0 %collective-permute-start.7 = (bf16[2,512,128]{2,1,0:T(8,128)(2,1)S(1)}, bf16[2,512,128]{2,1,0:T(8,128)(2,1)}, u32[]{:S(2)}, u32[]{:S(2)}) collective-permute-start(bf16[2,512,128]{2,1,0:T(8,128)(2,1)S(1)} %get-tuple-element.54), channel_id=1, source_target_pairs={{0,5},{1,4},{2,7},{3,6},{4,1},{5,0},{6,3},{7,2},{8,13},{9,12},{10,... | collective-permute-start | bytes 786440 | tf_op jit(solution)/shard_map/ppermute | solution.py:283
  49.2 8.0 %collective-permute-start.4 = (bf16[2,2,512,128]{3,2,1,0:T(8,128)(2,1)S(1)}, bf16[2,2,512,128]{3,2,1,0:T(8,128)(2,1)S(1)}, u32[]{:S(2)}, u32[]{:S(2)}) collective-permute-start(bf16[2,2,512,128]{3,2,1,0:T(8,128)(2,1)S(1)} %collective-permute-done.3.rest_2_), channel_id=1, source_target_pairs={{0,1},{1,0},{2,3},{3,2},{4,5},{5,4},{6,7},{7,6},{8,9},{9,8},{10,11... | collective-permute-start | bytes 1572872 | tf_op jit(solution)/shard_map/ppermute | solution.py:283
  53.0 1.0 %copy-start.3 = (bf16[2,512,128]{2,1,0:T(8,128)(2,1)S(1)}, bf16[2,512,128]{2,1,0:T(8,128)(2,1)}, u32[]{:S(2)}) copy-start(bf16[2,512,128]{2,1,0:T(8,128)(2,1)} %copy-done.2) | copy-start | bytes 786436
  77.9 14.2 %collective-permute-start.8 = (bf16[17,16,128]{2,1,0:T(8,128)(2,1)S(1)}, bf16[17,16,128]{2,1,0:T(8,128)(2,1)S(1)}, u32[]{:S(2)}, u32[]{:S(2)}) collective-permute-start(bf16[17,16,128]{2,1,0:T(8,128)(2,1)S(1)} %get-tuple-element.57), channel_id=1, source_target_pairs={{0,64},{1,65},{2,66},{3,67},{4,68},{5,69},{6,70},{7,71},{8,72},{9,... | collective-permute-start | bytes 208904 | tf_op jit(solution)/shard_map/ppermute | solution.py:283

commit v5 on v3

--- a/solution.py
+++ b/solution.py
@@ -319,8 +319,8 @@
     arrived, local, local_lse = lax.optimization_barrier((arrived, local, local_lse))
     packed, index = pack_queries(live.reshape(-1).astype(jnp.int32), arrived)
     near_beside = moved(near, 0, 1)
-    state = attend_stage(index, packed, (), [own, beside, far[0]], (None,) * 3)
-    state = attend_stage(index, packed, state, [near, near_beside, *far[1:3]], (0, 1, None, None))
+    state = attend_stage(index, packed, (), [own, beside, *far[:2]], (None,) * 4)
+    state = attend_stage(index, packed, state, [near, near_beside, far[2]], (0, 1, None))
     partial = attend_late(arrived.shape, index, packed, state, far[3:])
 
     returned = windowed(partial)

time: 94.1 us -> 95.3 us (1.013)
  the two profiles are of different devices: /device:TPU:128 before, /device:TPU:1 now
where the time goes in v5:
time: 95.3 us; the launch traced here: 94.3 us
  starting transfers between devices  49.9 us (52%)
  waiting for transfers between devices  14.1 us (15%)
  blocking collectives  12.8 us (13%)
  Pallas kernels  9.47 us (10%)
  local copies, waits for them, and re-layouts  5.39 us (6%)
  other arithmetic  2.29 us (2%)
    ppermute x9, starting transfers between devices, moved(): return lax.ppermute(x, ('group', 'tensor'), pairs)  45.5 us
    ppermute x9, waiting for transfers between devices, moved(): return lax.ppermute(x, ('group', 'tensor'), pairs)  14.1 us
    all_to_all x1, blocking collectives, windowed(): lax.all_to_all(x, 'group', 0, 0, axis_index_groups=windows, tiled=True)  12.8 us
    all_to_all x1, starting transfers between devices, windowed(): lax.all_to_all(x, 'group', 0, 0, axis_index_groups=windows, tiled=True)  4.48 us
    pallas_call x2, Pallas kernels, attend_stage(): pl.pallas_call(functools.partial(stage_kernel, len(state) // 2, halves),...  3.96 us
    optimization_barrier x2, local copies, waits for them, and re-layouts, on_device(): lax.optimization_barrier((own_kv, new_kv, far[3], cell))  2.11 us
  transfers between devices with their start and end apart: 10, of which 3 were waited for; matrix products, arithmetic and copies ran while one was open for 5% of the time, Pallas kernels for 7%

profile of v5, /device:TPU:1, one launch (start us, length us, event | category | flops | bytes accessed | tf_op | source)
XLA Modules:
  0.0 94.3 jit_solution(11961242989570551353)
XLA Ops:
  0.0 0.0 copy-start
  0.0 0.0 copy-start.1
  0.0 1.6 %copy-done.1 = bf16[1,512,2,8,128]{4,3,2,1,0:T(8,128)(2,1)S(1)} copy-done((bf16[1,512,2,8,128]{4,3,2,1,0:T(8,128)(2,1)S(1)}, bf16[1,512,2,8,128]{4,3,2,1,0:T(8,128)(2,1)}, u32[]{:S(2)}) %copy-start.1) | copy-done | bytes 2097176
  1.6 0.0 copy-start.3
  1.6 1.0 %split_prefix.1 = (bf16[2,512,128]{2,1,0:T(8,128)(2,1)S(1)}, bf16[2,512,128]{2,1,0:T(8,128)(2,1)S(1)}, bf16[2,2,512,128]{3,2,1,0:T(8,128)(2,1)S(1)}, bf16[2,512,...) custom-call(s32[1]{0:T(128)} %bitcast.lane_ref, ...), custom_call_target="tpu_custom_call" | custom-call | bytes 4194304 | tf_op jit(solution)/shard_map/split_prefix/pallas_call | solution.py:263
  2.6 8.8 %collective-permute-start = (bf16[2,512,128]{2,1,0:T(8,128)(2,1)S(1)}, bf16[2,512,128]{2,1,0:T(8,128)(2,1)S(1)}, u32[]{:S(2)}, u32[]{:S(2)}) collective-permute-start(bf16[2,512,128]{2,1,0:T(8,128)(2,1)S(1)} %get-tuple-element.31), channel_id=1, source_target_pairs={{0,1},{1,0},{2,3},{3,2},{4,5},{5,4},{6,7},{7,6},{8,9},{9,8},{10,11... | collective-permute-start | bytes 786440 | tf_op jit(solution)/shard_map/ppermute | solution.py:283
  11.4 1.9 %collective-permute-start.2 = (bf16[2,512,128]{2,1,0:T(8,128)(2,1)S(1)}, bf16[2,512,128]{2,1,0:T(8,128)(2,1)S(1)}, u32[]{:S(2)}, u32[]{:S(2)}) collective-permute-start(bf16[2,512,128]{2,1,0:T(8,128)(2,1)S(1)} %get-tuple-element.34), channel_id=1, source_target_pairs={{0,4},{1,5},{2,6},{3,7},{4,0},{5,1},{6,2},{7,3},{8,12},{9,13},{10,... | collective-permute-start | bytes 786440 | tf_op jit(solution)/shard_map/ppermute | solution.py:283
  13.3 4.4 %collective-permute-start.3 = (bf16[2,512,128]{2,1,0:T(8,128)(2,1)S(1)}, bf16[2,512,128]{2,1,0:T(8,128)(2,1)}, u32[]{:S(2)}, u32[]{:S(2)}) collective-permute-start(bf16[2,512,128]{2,1,0:T(8,128)(2,1)S(1)} %get-tuple-element.47), channel_id=1, source_target_pairs={{0,5},{1,4},{2,7},{3,6},{4,1},{5,0},{6,3},{7,2},{8,13},{9,12},{10,... | collective-permute-start | bytes 786440 | tf_op jit(solution)/shard_map/ppermute | solution.py:283
  17.8 1.9 %collective-permute-start.4 = (bf16[2,2,512,128]{3,2,1,0:T(8,128)(2,1)S(1)}, bf16[2,2,512,128]{3,2,1,0:T(8,128)(2,1)S(1)}, u32[]{:S(2)}, u32[]{:S(2)}) collective-permute-start(bf16[2,2,512,128]{3,2,1,0:T(8,128)(2,1)S(1)} %get-tuple-element.50), channel_id=1, source_target_pairs={{0,2},{1,3},{2,0},{3,1},{4,6},{5,7},{6,4},{7,5},{8,10},{9,11},{10,... | collective-permute-start | bytes 1572872 | tf_op jit(solution)/shard_map/ppermute | solution.py:283
  19.7 0.7 compare_select_fusion
  20.4 0.0 copy-done
  20.4 0.7 gather_fusion
  21.1 0.0 copy-done.3
  21.1 0.1 eq.17
  21.2 0.1 eq.18
  21.3 0.1 broadcast_in_dim.47
  21.4 0.0 collective-permute-done.rest_1_
  21.4 10.1 %collective-permute-start.1 = (bf16[17,16,128]{2,1,0:T(8,128)(2,1)S(1)}, bf16[17,16,128]{2,1,0:T(8,128)(2,1)S(1)}, u32[]{:S(2)}, u32[]{:S(2)}) collective-permute-start(bf16[17,16,128]{2,1,0:T(8,128)(2,1)S(1)} %pad_maximum_fusion), channel_id=1, source_target_pairs={{0,448},{1,449},{2,450},{3,451},{4,452},{5,453},{6,454},{7,455},{8... | collective-permute-start | bytes 208904 | tf_op jit(solution)/shard_map/ppermute | solution.py:283
  31.5 0.2 collective-permute-done.2.rest_2_
  31.7 3.9 %collective-permute-start.6 = (bf16[2,512,128]{2,1,0:T(8,128)(2,1)S(1)}, bf16[2,512,128]{2,1,0:T(8,128)(2,1)}, u32[]{:S(2)}, u32[]{:S(2)}) collective-permute-start(bf16[2,512,128]{2,1,0:T(8,128)(2,1)S(1)} %get-tuple-element.51), channel_id=1, source_target_pairs={{0,6},{1,7},{2,4},{3,5},{4,2},{5,3},{6,0},{7,1},{8,14},{9,15},{10,... | collective-permute-start | bytes 786440 | tf_op jit(solution)/shard_map/ppermute | solution.py:283
  35.6 0.0 collective-permute-done.1
  35.6 0.9 broadcast_select_fusion
  36.5 4.5 %all-to-all-start = ((bf16[8,17,16,128]{3,2,1,0:T(8,128)(2,1)}), bf16[8,17,16,128]{3,2,1,0:T(8,128)(2,1)S(1)}, u32[]{:S(2)}, u32[]{:S(2)}) async-start(bf16[8,17,16,128]{3,2,1,0:T(8,128)(2,1)} %broadcast_select_fusion), calls=%async_computation | async-start | bytes 1114112 | tf_op jit(solution)/shard_map/all_to_all | solution.py:289
  41.0 0.0 copy-start.4
  41.0 2.1 %copy.10 = bf16[16,256,2,128]{3,1,2,0:T(8,128)(2,1)S(1)} copy(bf16[16,256,2,128]{3,2,1,0:T(2,128)(2,1)} %param.9) | data formatting | bytes 4194304 | tf_op jit(solution)/shard_map/optimization_barrier | solution.py:315
  43.1 0.0 copy-done.4
  43.1 0.0 copy-start.2
  43.2 3.9 %collective-permute-start.7 = (bf16[2,512,128]{2,1,0:T(8,128)(2,1)S(1)}, bf16[2,512,128]{2,1,0:T(8,128)(2,1)}, u32[]{:S(2)}, u32[]{:S(2)}) collective-permute-start(bf16[2,512,128]{2,1,0:T(8,128)(2,1)S(1)} %get-tuple-element.54), channel_id=1, source_target_pairs={{0,7},{1,6},{2,5},{3,4},{4,3},{5,2},{6,1},{7,0},{8,15},{9,14},{10,... | collective-permute-start | bytes 786440 | tf_op jit(solution)/shard_map/ppermute | solution.py:283
  47.1 0.2 fusion.3.kv_ref
  47.3 0.0 copy-done.2
  47.3 1.2 %local_attention.1 = (f32[16,16,128]{2,1,0:T(8,128)S(1)}, f32[16,16,128]{2,1,0:T(8,128)S(1)}) custom-call(s32[16]{0:T(128)S(1)} %copy-done.2, bf16[16,16,128]{2,1,0:T(8,128)(2,1)S(1)} %reshape.51.q_ref, bf16[16,2,272,128]{3,2,1,0:T(8,128)(2,1)S(1)} %fusion.3.kv_ref), custom_call_target="tpu_custom_call" | custom-call | flops 20000000000 | bytes 2500000 | tf_op jit(solution)/shard_map/local_attention/pallas_call | solution.py:53
  48.5 1.2 %collective-permute-done.4.rest_2_ = bf16[2,2,512,128]{3,2,1,0:T(8,128)(2,1)S(1)} collective-permute-done((bf16[2,2,512,128]{3,2,1,0:T(8,128)(2,1)S(1)}, bf16[2,2,512,128]{3,2,1,0:T(8,128)(2,1)S(1)}, u32[]{:S(2)}, u32[]{:S(2)}) %collective-permute-start.4) | collective-permute-done | bytes 524320 | tf_op jit(solution)/shard_map/ppermute | solution.py:283
  49.7 8.5 %collective-permute-start.5 = (bf16[2,2,512,128]{3,2,1,0:T(8,128)(2,1)S(1)}, bf16[2,2,512,128]{3,2,1,0:T(8,128)(2,1)S(1)}, u32[]{:S(2)}, u32[]{:S(2)}) collective-permute-start(bf16[2,2,512,128]{3,2,1,0:T(8,128)(2,1)S(1)} %collective-permute-done.4.rest_2_), channel_id=1, source_target_pairs={{0,1},{1,0},{2,3},{3,2},{4,5},{5,4},{6,7},{7,6},{8,9},{9,8},{10,11... | collective-permute-start | bytes 1572872 | tf_op jit(solution)/shard_map/ppermute | solution.py:283
  58.3 0.0 all-to-all-done.q_ref
  58.3 0.2 convert_reduce_fusion
  58.5 0.1 reshape.53
  58.6 1.5 %pack_queries.1 = (bf16[144,16,128]{2,1,0:T(8,128)(2,1)S(1)}, s32[130]{0:T(256)S(1)}) custom-call(s32[128]{0:T(128)S(1)} %and_convert_fusion.live_ref, bf16[8,17,16,128]{3,2,1,0:T(8,128)(2,1)S(1)} %all-to-all-done.q_ref), custom_call_target="tpu_custom_call" | custom-call | tf_op jit(solution)/shard_map/pack_queries/pallas_call | solution.py:102
  60.1 0.0 collective-permute-done.3.rest_3_
  60.1 2.1 %attend_stage.2 = (f32[8,256,128]{2,1,0:T(8,128)S(1)}, f32[8,256,128]{2,1,0:T(8,128)S(1)}) custom-call(s32[130]{0:T(256)S(1)} %get-tuple-element.42.index, bf16[144,16,128]{2,1,0:T(8,128)(2,1)S(1)} %get-tuple-element.43.packed, bf16[2,512,128]{2,1,0:T(8,128)(2,1)S(1)} %get-tuple-element.44.rest_0_, bf16[2,512,128]{2,1,0:T(8,128)(2,1)S(1)} %collective-permute-done.rest_1_, ...), custom_call_target="tpu_custom_call" | custom-call | flops 10000000000 | bytes 2000000 | tf_op jit(solution)/shard_map/attend_stage/pallas_call | solution.py:145
  62.2 0.0 collective-permute-done.6.rest_4_
  62.2 0.0 collective-permute-done.5.rest_3_
  62.2 1.9 %attend_stage.3 = (f32[8,256,128]{2,1,0:T(8,128)S(1)}, f32[8,256,128]{2,1,0:T(8,128)S(1)}) custom-call(s32[130]{0:T(256)S(1)} %get-tuple-element.42.index, bf16[144,16,128]{2,1,0:T(8,128)(2,1)S(1)} %get-tuple-element.43.packed, f32[8,256,128]{2,1,0:T(8,128)S(1)} %get-tuple-element.48.rest_0_, f32[8,256,128]{2,1,0:T(8,128)S(1)} %get-tuple-element.49.rest_1_, ...), custom_call_target="tpu_custom_call" | custom-call | flops 10000000000 | bytes 2000000 | tf_op jit(solution)/shard_map/attend_stage/pallas_call | solution.py:145
  64.1 0.0 collective-permute-done.7.rest_0_
  64.1 1.6 %attend_late.1 = bf16[8,17,16,128]{3,2,1,0:T(8,128)(2,1)S(1)} custom-call(s32[130]{0:T(256)S(1)} %get-tuple-element.42.index, bf16[144,16,128]{2,1,0:T(8,128)(2,1)S(1)} %get-tuple-element.43.packed, f32[8,256,128]{2,1,0:T(8,128)S(1)} %get-tuple-element.52.attended_ref, f32[8,256,128]{2,1,0:T(8,128)S(1)} %get-tuple-element.53.level_ref, ...), custom_call_target="tpu_custom_call" | custom-call | flops 10000000000 | bytes 4000000 | tf_op jit(solution)/shard_map/attend_late/pallas_call | solution.py:199
  65.8 12.8 %all_to_all.10 = bf16[8,17,16,128]{3,2,1,0:T(8,128)(2,1)S(1)} all-to-all(bf16[8,17,16,128]{3,2,1,0:T(8,128)(2,1)S(1)} %attend_late.1), channel_id=1, replica_groups={{0,8,16,24,32,40,48,56},{64,72,80,88,96,104,112,120},{128,136,144,152,1..., dimensions={0} | all-to-all | bytes 1114112 | tf_op jit(solution)/shard_map/all_to_all | solution.py:289
  78.6 0.3 select_reduce_fusion
  78.8 1.9 %collective-permute-start.8 = (bf16[17,16,128]{2,1,0:T(8,128)(2,1)S(1)}, bf16[17,16,128]{2,1,0:T(8,128)(2,1)S(1)}, u32[]{:S(2)}, u32[]{:S(2)}) collective-permute-start(bf16[17,16,128]{2,1,0:T(8,128)(2,1)S(1)} %get-tuple-element.57), channel_id=1, source_target_pairs={{0,64},{1,65},{2,66},{3,67},{4,68},{5,69},{6,70},{7,71},{8,72},{9,... | collective-permute-start | bytes 208904 | tf_op jit(solution)/shard_map/ppermute | solution.py:283
  80.8 12.7 %collective-permute-done.8.refs_1_ = bf16[17,16,128]{2,1,0:T(8,128)(2,1)S(1)} collective-permute-done((bf16[17,16,128]{2,1,0:T(8,128)(2,1)S(1)}, bf16[17,16,128]{2,1,0:T(8,128)(2,1)S(1)}, u32[]{:S(2)}, u32[]{:S(2)}) %collective-permute-start.8) | collective-permute-done | bytes 69664 | tf_op jit(solution)/shard_map/ppermute | solution.py:283
  93.5 0.1 merge_parts.1
  93.6 0.7 reshape.52
  (8 shorter events, 0.1 us)
Async XLA Ops:
  0.0 20.4 %copy-start = (s32[64]{0:T(128)S(1)}, s32[64]{0:T(128)}, u32[]{:S(2)}) copy-start(s32[64]{0:T(128)} %param.11) | copy-start | bytes 772
  0.0 1.6 %copy-start.1 = (bf16[1,512,2,8,128]{4,3,2,1,0:T(8,128)(2,1)S(1)}, bf16[1,512,2,8,128]{4,3,2,1,0:T(8,128)(2,1)}, u32[]{:S(2)}) copy-start(bf16[1,512,2,8,128]{4,3,2,1,0:T(8,128)(2,1)} %param.10) | copy-start | bytes 6291460
  1.6 19.5 %copy-start.3 = (bf16[16,2,1024]{2,1,0:T(2,128)(2,1)S(1)}, bf16[16,2,1024]{2,1,0:T(2,128)(2,1)}, u32[]{:S(2)}) copy-start(bf16[16,2,1024]{2,1,0:T(2,128)(2,1)} %param.7) | copy-start | bytes 196612
  2.6 18.8 %collective-permute-start = (bf16[2,512,128]{2,1,0:T(8,128)(2,1)S(1)}, bf16[2,512,128]{2,1,0:T(8,128)(2,1)S(1)}, u32[]{:S(2)}, u32[]{:S(2)}) collective-permute-start(bf16[2,512,128]{2,1,0:T(8,128)(2,1)S(1)} %get-tuple-element.31), channel_id=1, source_target_pairs={{0,1},{1,0},{2,3},{3,2},{4,5},{5,4},{6,7},{7,6},{8,9},{9,8},{10,11... | collective-permute-start | bytes 786440 | tf_op jit(solution)/shard_map/ppermute | solution.py:283
  11.4 20.3 %collective-permute-start.2 = (bf16[2,512,128]{2,1,0:T(8,128)(2,1)S(1)}, bf16[2,512,128]{2,1,0:T(8,128)(2,1)S(1)}, u32[]{:S(2)}, u32[]{:S(2)}) collective-permute-start(bf16[2,512,128]{2,1,0:T(8,128)(2,1)S(1)} %get-tuple-element.34), channel_id=1, source_target_pairs={{0,4},{1,5},{2,6},{3,7},{4,0},{5,1},{6,2},{7,3},{8,12},{9,13},{10,... | collective-permute-start | bytes 786440 | tf_op jit(solution)/shard_map/ppermute | solution.py:283
  13.3 46.8 %collective-permute-start.3 = (bf16[2,512,128]{2,1,0:T(8,128)(2,1)S(1)}, bf16[2,512,128]{2,1,0:T(8,128)(2,1)}, u32[]{:S(2)}, u32[]{:S(2)}) collective-permute-start(bf16[2,512,128]{2,1,0:T(8,128)(2,1)S(1)} %get-tuple-element.47), channel_id=1, source_target_pairs={{0,5},{1,4},{2,7},{3,6},{4,1},{5,0},{6,3},{7,2},{8,13},{9,12},{10,... | collective-permute-start | bytes 786440 | tf_op jit(solution)/shard_map/ppermute | solution.py:283
  17.8 32.0 %collective-permute-start.4 = (bf16[2,2,512,128]{3,2,1,0:T(8,128)(2,1)S(1)}, bf16[2,2,512,128]{3,2,1,0:T(8,128)(2,1)S(1)}, u32[]{:S(2)}, u32[]{:S(2)}) collective-permute-start(bf16[2,2,512,128]{3,2,1,0:T(8,128)(2,1)S(1)} %get-tuple-element.50), channel_id=1, source_target_pairs={{0,2},{1,3},{2,0},{3,1},{4,6},{5,7},{6,4},{7,5},{8,10},{9,11},{10,... | collective-permute-start | bytes 1572872 | tf_op jit(solution)/shard_map/ppermute | solution.py:283
  21.4 14.2 %collective-permute-start.1 = (bf16[17,16,128]{2,1,0:T(8,128)(2,1)S(1)}, bf16[17,16,128]{2,1,0:T(8,128)(2,1)S(1)}, u32[]{:S(2)}, u32[]{:S(2)}) collective-permute-start(bf16[17,16,128]{2,1,0:T(8,128)(2,1)S(1)} %pad_maximum_fusion), channel_id=1, source_target_pairs={{0,448},{1,449},{2,450},{3,451},{4,452},{5,453},{6,454},{7,455},{8... | collective-permute-start | bytes 208904 | tf_op jit(solution)/shard_map/ppermute | solution.py:283
  31.7 30.5 %collective-permute-start.6 = (bf16[2,512,128]{2,1,0:T(8,128)(2,1)S(1)}, bf16[2,512,128]{2,1,0:T(8,128)(2,1)}, u32[]{:S(2)}, u32[]{:S(2)}) collective-permute-start(bf16[2,512,128]{2,1,0:T(8,128)(2,1)S(1)} %get-tuple-element.51), channel_id=1, source_target_pairs={{0,6},{1,7},{2,4},{3,5},{4,2},{5,3},{6,0},{7,1},{8,14},{9,15},{10,... | collective-permute-start | bytes 786440 | tf_op jit(solution)/shard_map/ppermute | solution.py:283
  36.5 21.7 %all-to-all-start = ((bf16[8,17,16,128]{3,2,1,0:T(8,128)(2,1)}), bf16[8,17,16,128]{3,2,1,0:T(8,128)(2,1)S(1)}, u32[]{:S(2)}, u32[]{:S(2)}) async-start(bf16[8,17,16,128]{3,2,1,0:T(8,128)(2,1)} %broadcast_select_fusion), calls=%async_computation | async-start | bytes 1114112 | tf_op jit(solution)/shard_map/all_to_all | solution.py:289
  41.0 2.1 %copy-start.4 = (bf16[16,2,2,128]{3,2,1,0:T(2,128)(2,1)S(1)}, bf16[16,2,2,128]{3,2,1,0:T(2,128)(2,1)}, u32[]{:S(2)}) copy-start(bf16[16,2,2,128]{3,2,1,0:T(2,128)(2,1)} %param.8) | copy-start | bytes 49156
  43.1 4.1 %copy-start.2 = (s32[16]{0:T(128)S(1)}, s32[16]{0:T(128)}, u32[]{:S(2)}) copy-start(s32[16]{0:T(128)} %len_ref.1) | copy-start | bytes 196
  43.2 20.9 %collective-permute-start.7 = (bf16[2,512,128]{2,1,0:T(8,128)(2,1)S(1)}, bf16[2,512,128]{2,1,0:T(8,128)(2,1)}, u32[]{:S(2)}, u32[]{:S(2)}) collective-permute-start(bf16[2,512,128]{2,1,0:T(8,128)(2,1)S(1)} %get-tuple-element.54), channel_id=1, source_target_pairs={{0,7},{1,6},{2,5},{3,4},{4,3},{5,2},{6,1},{7,0},{8,15},{9,14},{10,... | collective-permute-start | bytes 786440 | tf_op jit(solution)/shard_map/ppermute | solution.py:283
  49.7 12.5 %collective-permute-start.5 = (bf16[2,2,512,128]{3,2,1,0:T(8,128)(2,1)S(1)}, bf16[2,2,512,128]{3,2,1,0:T(8,128)(2,1)S(1)}, u32[]{:S(2)}, u32[]{:S(2)}) collective-permute-start(bf16[2,2,512,128]{3,2,1,0:T(8,128)(2,1)S(1)} %collective-permute-done.4.rest_2_), channel_id=1, source_target_pairs={{0,1},{1,0},{2,3},{3,2},{4,5},{5,4},{6,7},{7,6},{8,9},{9,8},{10,11... | collective-permute-start | bytes 1572872 | tf_op jit(solution)/shard_map/ppermute | solution.py:283
  78.8 14.6 %collective-permute-start.8 = (bf16[17,16,128]{2,1,0:T(8,128)(2,1)S(1)}, bf16[17,16,128]{2,1,0:T(8,128)(2,1)S(1)}, u32[]{:S(2)}, u32[]{:S(2)}) collective-permute-start(bf16[17,16,128]{2,1,0:T(8,128)(2,1)S(1)} %get-tuple-element.57), channel_id=1, source_target_pairs={{0,64},{1,65},{2,66},{3,67},{4,68},{5,69},{6,70},{7,71},{8,72},{9,... | collective-permute-start | bytes 208904 | tf_op jit(solution)/shard_map/ppermute | solution.py:283
